TPU v7x, 512 devices: a whole 4x8x8 slice. The times are simulated.
512 devices in a mesh: leaf: 128 (over z, y, core), near: 4 (over x).
Axes of the slice: x: 4, y: 8, z: 8, core: 2. Of those that a mesh axis runs over, the one named last changes fastest.
Arguments:
- positions: float32 [3, 3072, 512], P(None, 'leaf', 'near'), may hold values from 0 to 1
- noise_variance: float32 [3072, 512], P('leaf', 'near'), may hold values from 0.5 to 2
- solution: float32 [3072, 512], P('leaf', 'near'), may hold values from -6 to 6
- residual: float32 [3072, 512], P('leaf', 'near'), may hold values from -6 to 6
- direction: float32 [3072, 512], P('leaf', 'near'), may hold values from -6 to 6
- leaf_basis: float32 [3072, 64, 512], P('leaf', None, 'near'), may hold values from -0.25 to 0.25
- leaf_skeleton: float32 [3, 3072, 64], P(None, 'leaf'), may hold values from 0 to 1
- leaf_transfer: float32 [3072, 64, 64], P('leaf'), may hold values from -0.75 to 0.75
- box_transfer: float32 [128, 5, 64, 64], P('leaf'), may hold values from -0.75 to 0.75
- box_skeleton: float32 [3, 128, 6, 64], P(None, 'leaf'), may hold values from 0 to 1
- leaf_count: int32 [128], P('leaf'), may hold values from 1 to 24, as said below
- near_list: int32 [3072, 9], P('leaf'), may hold values from -1 to 71, as said below
- far_list: int32 [3072, 8], P('leaf', 'near'), may hold values from -1 to 71, as said below
Outputs:
- new_solution: float32 [3072, 512], P('leaf', 'near')
- new_residual: float32 [3072, 512], P('leaf', 'near')
- new_direction: float32 [3072, 512], P('leaf', 'near')
Inputs may be any that keep to these rules, and one draw needn't show every extreme that they name: `leaf_count`: at least one leaf group holds 24 leaves and at least one holds 1, in every draw; a few groups are full, and the others hold up to two thirds of 24. `near_list`: entry 0 is the slot itself; the other entries name distinct occupied slots of the window, or are -1. Slots outside the mesh's first and last groups are never named. `far_list`: entries name distinct occupied slots of the window that are not in the slot's near list, or are -1.
All inputs are finite; a program needn't handle non-finite values.
Results may differ from a plain program's by a relative error of at most 0.0003.
Values sent between devices are 32-bit elements; how exact they have to be, the bound alone decides.
A program may use at most 64 MiB of HBM per device.

v0:
```python
import jax
import jax.numpy as jnp
from jax import lax
from jax.sharding import PartitionSpec as P

AMPLITUDE = 0.02
LENGTH = 0.5
HIGHEST = lax.Precision.HIGHEST


def padded(shard, sides, width):
    for axis, dim in sides:
        count, length = (lax.axis_size(axis), shard.shape[dim])
        up = [(i, (i + 1) % count) for i in range(count - 1)]
        down = [(j, i) for i, j in up]
        last = lax.slice_in_dim(shard, length - width, length, axis=dim)
        first = lax.slice_in_dim(shard, 0, width, axis=dim)
        before = lax.ppermute(last, axis, up)
        after = lax.ppermute(first, axis, down)
        shard = jnp.concatenate([before, shard, after], axis=dim)
    return shard


def passed_along(shard, axis, by):
    count = lax.axis_size(axis)
    pairs = [(i, i + by) for i in range(count) if 0 <= i + by < count]
    return lax.ppermute(shard, axis, pairs)


def kernel_block(targets, sources):
    squared = None
    for component in range(3):
        spacing = targets[component][..., :, None] - sources[component][..., None, :]
        squared = spacing * spacing if squared is None else squared + spacing * spacing
    return AMPLITUDE * jnp.exp(-jnp.sqrt(squared) / LENGTH)


def near_field(targets, window, near_list):
    capacity = targets.shape[1]
    target_rows = targets.shape[2]
    groups = capacity // 4
    grouped = targets.reshape(3, groups, 4, target_rows).transpose(1, 0, 2, 3)
    listing = near_list.reshape(groups, 4, near_list.shape[1])

    def one_group(items):
        group_targets, group_lists = items
        running = jnp.zeros((4, target_rows), jnp.float32)
        for listed in range(group_lists.shape[1]):
            indices = group_lists[:, listed]
            present = indices >= 0
            sources = jnp.take(window, jnp.maximum(indices, 0), axis=1)
            weights = jnp.where(present[:, None], sources[3], 0.0)
            kernel_tile = kernel_block(group_targets, sources[:3])
            running = running + jnp.sum(kernel_tile * weights[:, None, :], axis=2)
        return running

    result = lax.map(one_group, (grouped, listing))
    return result.reshape(capacity, target_rows)


def per_device(
    positions,
    noise_variance,
    solution,
    residual,
    direction,
    leaf_basis,
    leaf_skeleton,
    leaf_transfer,
    box_transfer,
    box_skeleton,
    leaf_count,
    near_list,
    far_list,
):
    capacity = positions.shape[1]
    occupied = (jnp.arange(capacity, dtype=jnp.int32) < leaf_count[0])[:, None]
    masked_direction = jnp.where(occupied, direction, 0.0)
    masked_residual = jnp.where(occupied, residual, 0.0)
    masked_solution = jnp.where(occupied, solution, 0.0)
    norm_old = lax.psum(jnp.sum(masked_residual * masked_residual), ("leaf", "near"))
    packed = jnp.concatenate([positions, masked_direction[None]], axis=0)
    whole_leaves = lax.all_gather(packed, "near", axis=2, tiled=True)
    window = padded(whole_leaves, (("leaf", 1),), capacity)
    near_term = near_field(positions, window, near_list)
    coeffs = lax.psum(
        jnp.einsum("srp,sp->sr", leaf_basis, masked_direction, precision=HIGHEST), "near"
    )
    far_window_data = padded(
        jnp.concatenate([leaf_skeleton, coeffs[None]], axis=0), (("leaf", 1),), capacity
    )
    partial_far = jnp.zeros_like(coeffs)
    for listed in range(far_list.shape[1]):
        indices = far_list[:, listed]
        present = indices >= 0
        sources = jnp.take(far_window_data, jnp.maximum(indices, 0), axis=1)
        weights = jnp.where(present[:, None], sources[3], 0.0)
        kernel_tile = kernel_block(leaf_skeleton, sources[:3])
        partial_far = partial_far + jnp.einsum(
            "sxy,sy->sx", kernel_tile, weights, precision=HIGHEST
        )
    far_local = lax.psum(partial_far, "near")
    levels = lax.axis_size("leaf").bit_length() - 2
    position = lax.axis_index("leaf")
    ascending = [jnp.einsum("sab,sb->a", leaf_transfer, coeffs, precision=HIGHEST)]
    for height in range(levels - 1):
        stride = 2**height
        lifted = jnp.dot(box_transfer[0, height], ascending[-1], precision=HIGHEST)
        partner = passed_along(lifted, "leaf", -stride)
        ascending.append(lifted + partner)
    local_fields = []
    for height in range(levels):
        stride = 2**height
        skeleton = box_skeleton[:, 0, height, :]
        payload = jnp.concatenate([skeleton, ascending[height][None]], axis=0)
        is_odd = position // stride % 2 == 1
        field = jnp.zeros_like(ascending[height])
        for offset in (-3, -2, 2, 3):
            incoming = passed_along(payload, "leaf", -offset * stride)
            kernel_tile = kernel_block(skeleton, incoming[:3])
            contribution = jnp.dot(kernel_tile, incoming[3], precision=HIGHEST)
            if offset == -3:
                contribution = jnp.where(is_odd, contribution, 0.0)
            elif offset == 3:
                contribution = jnp.where(is_odd, 0.0, contribution)
            field = field + contribution
        local_fields.append(field)
    downward = local_fields[levels - 1]
    for height in range(levels - 2, -1, -1):
        stride = 2**height
        received = passed_along(downward, "leaf", stride)
        is_odd = position // stride % 2 == 1
        parent = jnp.where(is_odd, received, downward)
        downward = local_fields[height] + jnp.dot(
            box_transfer[0, height].T, parent, precision=HIGHEST
        )
    expansion = far_local + jnp.einsum("sba,b->sa", leaf_transfer, downward, precision=HIGHEST)
    far_values = jnp.einsum("srp,sr->sp", leaf_basis, expansion, precision=HIGHEST)
    image = jnp.where(occupied, noise_variance * masked_direction + near_term + far_values, 0.0)
    curvature = lax.psum(jnp.sum(masked_direction * image), ("leaf", "near"))
    step_length = norm_old / curvature
    new_solution = masked_solution + step_length * masked_direction
    new_residual = masked_residual - step_length * image
    norm_new = lax.psum(jnp.sum(new_residual * new_residual), ("leaf", "near"))
    new_direction = new_residual + norm_new / norm_old * masked_direction
    return (new_solution, new_residual, new_direction)


def solution(mesh):
    return jax.shard_map(
        per_device,
        mesh=mesh,
        in_specs=(
            P(None, "leaf", "near"),
            P("leaf", "near"),
            P("leaf", "near"),
            P("leaf", "near"),
            P("leaf", "near"),
            P("leaf", None, "near"),
            P(None, "leaf", None),
            P("leaf", None, None),
            P("leaf", None, None, None),
            P(None, "leaf", None, None),
            P("leaf"),
            P("leaf", None),
            P("leaf", "near"),
        ),
        out_specs=(P("leaf", "near"), P("leaf", "near"), P("leaf", "near")),
        check_vma=False,
    )
```

profile of v0, /device:TPU:1, one launch (start us, length us, event | category | flops | bytes accessed | tf_op | source)
XLA Modules:
  0.0 613.3 jit_solution(4647885283070920641)
XLA Ops:
  2.2 1.3 fusion.753
  3.5 14.0 %psum.36 = f32[24,64]{1,0:T(8,128)S(1)} all-reduce(f32[24,64]{1,0:T(8,128)S(1)} %bitcast.808), channel_id=1, replica_groups=mesh['leaf'=128,'near'=4] {'near'}, use_global_device_ids=true, to_apply=%region_13.15 | all-reduce | flops 1536 | bytes 12288 | tf_op jit(solution)/shard_map/psum | solution.py:86
  18.4 1.3 collective-permute-start.7
  19.7 1.3 collective-permute-start.6
  21.0 11.7 %collective-permute-start.5 = (f32[4,64]{1,0:T(4,128)S(1)}, f32[4,64]{1,0:T(4,128)S(1)}, u32[]{:S(2)}, u32[]{:S(2)}) collective-permute-start(f32[4,64]{1,0:T(4,128)S(1)} %pad_maximum_fusion.4), channel_id=1, source_target_pairs={{0,8},{4,12},{8,16},{12,20},{16,24},{20,28},{24,32},{28,36},{32,40... | collective-permute-start | bytes 3080 | tf_op jit(solution)/shard_map/ppermute | solution.py:27
  32.7 2.0 collective-permute-start.4
  34.9 3.7 collective-permute-start.8
  40.3 10.1 %all_gather.3 = f32[4,24,512]{2,0,1:T(4,128)S(1)} all-gather(f32[4,24,128]{2,0,1:T(4,128)S(1)} %pad_maximum_fusion.2), channel_id=1, replica_groups=mesh['leaf'=128,'near'=4] {'near'}, dimensions={2}, use_global_device_ids=true | all-gather | bytes 245760 | tf_op jit(solution)/shard_map/all_gather | solution.py:83
  51.4 1.3 collective-permute-start.13
  52.7 3.0 collective-permute-done.13
  55.8 1.3 collective-permute-start.18
  57.2 3.9 collective-permute-done.18
  61.0 7.0 %collective-permute-start.2 = (f32[4,24,64]{2,0,1:T(4,128)S(1)}, f32[4,24,64]{2,0,1:T(4,128)S(1)}, u32[]{:S(2)}, u32[]{:S(2)}) collective-permute-start(f32[4,24,64]{2,0,1:T(4,128)S(1)} %pad_maximum_fusion.3), channel_id=1, source_target_pairs={{0,4},{4,8},{8,12},{12,16},{16,20},{20,24},{24,28},{28,32},{32,36}... | collective-permute-start | bytes 73736 | tf_op jit(solution)/shard_map/ppermute | solution.py:18
  68.3 1.9 collective-permute-start.3
  70.2 1.3 collective-permute-start.23
  71.5 6.9 %collective-permute-done.23 = f32[64]{0:T(128)S(1)} collective-permute-done((f32[64]{0:T(128)S(1)}, f32[64]{0:T(128)S(1)}, u32[]{:S(2)}, u32[]{:S(2)}) %collective-permute-start.23) | collective-permute-done | bytes 288 | tf_op jit(solution)/shard_map/ppermute | solution.py:27
  78.4 4.8 collective-permute-start
  83.2 1.9 collective-permute-start.1
  85.3 1.3 collective-permute-start.12
  87.5 5.7 collective-permute-done.12
  94.4 4.9 collective-permute-done.11
  99.4 5.5 collective-permute-start.10
  106.9 8.0 %collective-permute-done.28 = f32[64]{0:T(128)S(1)} collective-permute-done((f32[64]{0:T(128)S(1)}, f32[64]{0:T(128)S(1)}, u32[]{:S(2)}, u32[]{:S(2)}) %collective-permute-start.28) | collective-permute-done | bytes 288 | tf_op jit(solution)/shard_map/ppermute | solution.py:27
  119.0 9.3 %collective-permute-done.17 = f32[4,64]{1,0:T(4,128)S(1)} collective-permute-done((f32[4,64]{1,0:T(4,128)S(1)}, f32[4,64]{1,0:T(4,128)S(1)}, u32[]{:S(2)}, u32[]{:S(2)}) %collective-permute-start.17) | collective-permute-done | bytes 1056 | tf_op jit(solution)/shard_map/ppermute | solution.py:27
  129.6 6.9 %collective-permute-done.16 = f32[4,64]{1,0:T(4,128)S(1)} collective-permute-done((f32[4,64]{1,0:T(4,128)S(1)}, f32[4,64]{1,0:T(4,128)S(1)}, u32[]{:S(2)}, u32[]{:S(2)}) %collective-permute-start.16) | collective-permute-done | bytes 1056 | tf_op jit(solution)/shard_map/ppermute | solution.py:27
  136.5 6.7 %collective-permute-start.15 = (f32[4,64]{1,0:T(4,128)S(1)}, f32[4,64]{1,0:T(4,128)S(1)}, u32[]{:S(2)}, u32[]{:S(2)}) collective-permute-start(f32[4,64]{1,0:T(4,128)S(1)} %pad_maximum_fusion.6), channel_id=1, source_target_pairs={{0,32},{4,36},{8,40},{12,44},{16,48},{20,52},{24,56},{28,60},{32,6... | collective-permute-start | bytes 3080 | tf_op jit(solution)/shard_map/ppermute | solution.py:27
  144.0 7.7 %collective-permute-start.14 = (f32[4,64]{1,0:T(4,128)S(1)}, f32[4,64]{1,0:T(4,128)S(1)}, u32[]{:S(2)}, u32[]{:S(2)}) collective-permute-start(f32[4,64]{1,0:T(4,128)S(1)} %pad_maximum_fusion.6), channel_id=1, source_target_pairs={{0,48},{4,52},{8,56},{12,60},{16,64},{20,68},{24,72},{28,76},{32,8... | collective-permute-start | bytes 3080 | tf_op jit(solution)/shard_map/ppermute | solution.py:27
  154.5 13.8 %collective-permute-done.22 = f32[4,64]{1,0:T(4,128)S(1)} collective-permute-done((f32[4,64]{1,0:T(4,128)S(1)}, f32[4,64]{1,0:T(4,128)S(1)}, u32[]{:S(2)}, u32[]{:S(2)}) %collective-permute-start.22) | collective-permute-done | bytes 1056 | tf_op jit(solution)/shard_map/ppermute | solution.py:27
  168.3 4.6 collective-permute-start.20
  174.9 5.4 collective-permute-done.21
  180.3 10.3 %collective-permute-start.19 = (f32[4,64]{1,0:T(4,128)S(1)}, f32[4,64]{1,0:T(4,128)S(1)}, u32[]{:S(2)}, u32[]{:S(2)}) collective-permute-start(f32[4,64]{1,0:T(4,128)S(1)} %pad_maximum_fusion.7), channel_id=1, source_target_pairs={{0,96},{4,100},{8,104},{12,108},{16,112},{20,116},{24,120},{28,124... | collective-permute-start | bytes 3080 | tf_op jit(solution)/shard_map/ppermute | solution.py:27
  191.3 7.7 %collective-permute-start.25 = (f32[4,64]{1,0:T(4,128)S(1)}, f32[4,64]{1,0:T(4,128)S(1)}, u32[]{:S(2)}, u32[]{:S(2)}) collective-permute-start(f32[4,64]{1,0:T(4,128)S(1)} %pad_maximum_fusion.8), channel_id=1, source_target_pairs={{0,128},{4,132},{8,136},{12,140},{16,144},{20,148},{24,152},{28,15... | collective-permute-start | bytes 3080 | tf_op jit(solution)/shard_map/ppermute | solution.py:27
  199.9 1.3 collective-permute-start.26
  201.2 6.9 %collective-permute-done.26 = f32[4,64]{1,0:T(4,128)S(1)} collective-permute-done((f32[4,64]{1,0:T(4,128)S(1)}, f32[4,64]{1,0:T(4,128)S(1)}, u32[]{:S(2)}, u32[]{:S(2)}) %collective-permute-start.26) | collective-permute-done | bytes 1056 | tf_op jit(solution)/shard_map/ppermute | solution.py:27
  209.4 5.2 collective-permute-done.27
  214.6 6.4 %collective-permute-start.24 = (f32[4,64]{1,0:T(4,128)S(1)}, f32[4,64]{1,0:T(4,128)S(1)}, u32[]{:S(2)}, u32[]{:S(2)}) collective-permute-start(f32[4,64]{1,0:T(4,128)S(1)} %pad_maximum_fusion.8), channel_id=1, source_target_pairs={{0,192},{4,196},{8,200},{12,204},{16,208},{20,212},{24,216},{28,22... | collective-permute-start | bytes 3080 | tf_op jit(solution)/shard_map/ppermute | solution.py:27
  221.7 7.8 %collective-permute-start.30 = (f32[4,64]{1,0:T(4,128)S(1)}, f32[4,64]{1,0:T(4,128)S(1)}, u32[]{:S(2)}, u32[]{:S(2)}) collective-permute-start(f32[4,64]{1,0:T(4,128)S(1)} %pad_maximum_fusion.9), channel_id=1, source_target_pairs={{0,256},{4,260},{8,264},{12,268},{16,272},{20,276},{24,280},{28,28... | collective-permute-start | bytes 3080 | tf_op jit(solution)/shard_map/ppermute | solution.py:27
  230.3 1.3 collective-permute-start.31
  231.6 6.9 %collective-permute-done.31 = f32[4,64]{1,0:T(4,128)S(1)} collective-permute-done((f32[4,64]{1,0:T(4,128)S(1)}, f32[4,64]{1,0:T(4,128)S(1)}, u32[]{:S(2)}, u32[]{:S(2)}) %collective-permute-start.31) | collective-permute-done | bytes 1056 | tf_op jit(solution)/shard_map/ppermute | solution.py:27
  239.8 5.1 collective-permute-done.32
  244.9 1.7 collective-permute-start.29
  248.4 1.3 collective-permute-start.33
  250.5 2.6 collective-permute-start.34
  254.0 4.2 collective-permute-start.35
  259.0 1.3 collective-permute-start.36
  261.1 31.4 %collective-permute-start.37 = (f32[64]{0:T(128)S(1)}, f32[64]{0:T(128)S(1)}, u32[]{:S(2)}, u32[]{:S(2)}) collective-permute-start(f32[64]{0:T(128)S(1)} %fusion.27), channel_id=1, source_target_pairs={{0,4},{4,8},{8,12},{12,16},{16,20},{20,24},{24,28},{28,32},{32,36}... | collective-permute-start | bytes 776 | tf_op jit(solution)/shard_map/ppermute | solution.py:27
  295.5 2.1 fusion.75
  297.6 2.1 fusion.61
  299.7 11.0 %psum.37 = f32[24,64]{1,0:T(8,128)S(1)} all-reduce(f32[24,64]{1,0:T(8,128)S(1)} %add.452), channel_id=1, replica_groups=mesh['leaf'=128,'near'=4] {'near'}, use_global_device_ids=true, to_apply=%region_14.17 | all-reduce | flops 1536 | bytes 12288 | tf_op jit(solution)/shard_map/psum | solution.py:102
  311.7 87.9 %while.10 = (s32[]{:T(128)}, f32[6,4,128]{2,1,0:T(4,128)S(1)}, f32[6,3,4,128]{3,2,0,1:T(4,128)S(1)}, s32[6,4,9]{2,1,0:T(4,128)S(1)}, f32[4,72,512]{2,0,1:T(4,128)S(1)}, /*index=5*/s32[]{:T(128)}) while((s32[]{:T(128)}, f32[6,4,128]{2,1,0:T(4,128)S(1)}, f32[6,3,4,128]{3,2,0,1:T(4,128)S(1)}, s32[6,4,9]{2,1,0:T(4,128)S(1)}, ...), condition=%wide.region_12.14_spmd, body=%wide.region_2.13_spmd.sunk | while | flops 28431244 | bytes 2250369 | solution.py:57
  315.5 3.1 multiply_reduce_fusion.17
  321.6 3.0 multiply_reduce_fusion.16
  330.1 3.1 multiply_reduce_fusion.17
  336.3 3.0 multiply_reduce_fusion.16
  344.8 3.1 multiply_reduce_fusion.17
  350.9 3.0 multiply_reduce_fusion.16
  359.4 3.1 multiply_reduce_fusion.17
  365.6 3.0 multiply_reduce_fusion.16
  374.1 3.1 multiply_reduce_fusion.17
  380.2 3.0 multiply_reduce_fusion.16
  388.7 3.1 multiply_reduce_fusion.17
  394.9 3.0 multiply_reduce_fusion.16
  400.4 113.0 %all-reduce = (f32[]{:T(128)}, f32[]{:T(128)}) all-reduce(f32[]{:T(128)} %get-tuple-element.70, f32[]{:T(128)} %get-tuple-element.69), channel_id=1, replica_groups=mesh['leaf'=128,'near'=4] {'leaf','near'}, use_global_device_ids=true, to_apply=%region_1.2 | all-reduce | flops 2 | bytes 16 | tf_op jit(solution)/shard_map/psum | solution.py:81
  516.0 95.2 %psum.39 = f32[]{:T(128)} all-reduce(f32[]{:T(128)} %get-tuple-element.83), channel_id=1, replica_groups=mesh['leaf'=128,'near'=4] {'leaf','near'}, use_global_device_ids=true, to_apply=%region_18.21 | all-reduce | flops 1 | bytes 8 | tf_op jit(solution)/shard_map/psum | solution.py:144
  (550 shorter events, 87.0 us)
Async XLA Ops:
  0.6 1.6 copy-start
  0.6 17.0 %copy-start.1 = (f32[24,64,64]{2,1,0:T(8,128)S(1)}, f32[24,64,64]{2,1,0:T(8,128)}, u32[]{:S(2)}) copy-start(f32[24,64,64]{2,1,0:T(8,128)} %param.26) | copy-start | bytes 1179652
  3.5 14.1 %copy-start.9 = (f32[3,1,6,64]{3,1,2,0:T(1,128)S(1)}, f32[3,1,6,64]{3,1,2,0:T(1,128)}, u32[]{:S(2)}) copy-start(f32[3,1,6,64]{3,1,2,0:T(1,128)} %param.28) | copy-start | bytes 13828
  17.6 17.1 %copy-start.2 = (f32[1,5,64,64]{3,2,1,0:T(8,128)S(1)}, f32[1,5,64,64]{3,2,1,0:T(8,128)}, u32[]{:S(2)}) copy-start(f32[1,5,64,64]{3,2,1,0:T(8,128)} %param.27) | copy-start | bytes 245764
  18.4 49.9 %collective-permute-start.7 = (f32[4,64]{1,0:T(4,128)S(1)}, f32[4,64]{1,0:T(4,128)S(1)}, u32[]{:S(2)}, u32[]{:S(2)}) collective-permute-start(f32[4,64]{1,0:T(4,128)S(1)} %pad_maximum_fusion.4), channel_id=1, source_target_pairs={{12,0},{16,4},{20,8},{24,12},{28,16},{32,20},{36,24},{40,28},{44,3... | collective-permute-start | bytes 3080 | tf_op jit(solution)/shard_map/ppermute | solution.py:27
  19.7 50.5 %collective-permute-start.6 = (f32[4,64]{1,0:T(4,128)S(1)}, f32[4,64]{1,0:T(4,128)S(1)}, u32[]{:S(2)}, u32[]{:S(2)}) collective-permute-start(f32[4,64]{1,0:T(4,128)S(1)} %pad_maximum_fusion.4), channel_id=1, source_target_pairs={{8,0},{12,4},{16,8},{20,12},{24,16},{28,20},{32,24},{36,28},{40,32... | collective-permute-start | bytes 3080 | tf_op jit(solution)/shard_map/ppermute | solution.py:27
  21.0 62.2 %collective-permute-start.5 = (f32[4,64]{1,0:T(4,128)S(1)}, f32[4,64]{1,0:T(4,128)S(1)}, u32[]{:S(2)}, u32[]{:S(2)}) collective-permute-start(f32[4,64]{1,0:T(4,128)S(1)} %pad_maximum_fusion.4), channel_id=1, source_target_pairs={{0,8},{4,12},{8,16},{12,20},{16,24},{20,28},{24,32},{28,36},{32,40... | collective-permute-start | bytes 3080 | tf_op jit(solution)/shard_map/ppermute | solution.py:27
  32.7 52.6 %collective-permute-start.4 = (f32[4,64]{1,0:T(4,128)S(1)}, f32[4,64]{1,0:T(4,128)S(1)}, u32[]{:S(2)}, u32[]{:S(2)}) collective-permute-start(f32[4,64]{1,0:T(4,128)S(1)} %pad_maximum_fusion.4), channel_id=1, source_target_pairs={{0,12},{4,16},{8,20},{12,24},{16,28},{20,32},{24,36},{28,40},{32,4... | collective-permute-start | bytes 3080 | tf_op jit(solution)/shard_map/ppermute | solution.py:27
  34.9 16.4 %collective-permute-start.8 = (f32[64]{0:T(128)S(1)}, f32[64]{0:T(128)S(1)}, u32[]{:S(2)}, u32[]{:S(2)}) collective-permute-start(f32[64]{0:T(128)S(1)} %convolution_bitcast_fusion.29), channel_id=1, source_target_pairs={{4,0},{8,4},{12,8},{16,12},{20,16},{24,20},{28,24},{32,28},{36,32}... | collective-permute-start | bytes 776 | tf_op jit(solution)/shard_map/ppermute | solution.py:27
  38.7 0.8 copy-start.4
  38.7 0.7 copy-start.12
  39.5 0.8 copy-start.5
  50.5 0.7 copy-start.11
  51.4 4.3 collective-permute-start.13
  55.8 5.2 collective-permute-start.18
  61.0 232.8 %collective-permute-start.2 = (f32[4,24,64]{2,0,1:T(4,128)S(1)}, f32[4,24,64]{2,0,1:T(4,128)S(1)}, u32[]{:S(2)}, u32[]{:S(2)}) collective-permute-start(f32[4,24,64]{2,0,1:T(4,128)S(1)} %pad_maximum_fusion.3), channel_id=1, source_target_pairs={{0,4},{4,8},{8,12},{12,16},{16,20},{20,24},{24,28},{28,32},{32,36}... | collective-permute-start | bytes 73736 | tf_op jit(solution)/shard_map/ppermute | solution.py:18
  68.3 225.6 %collective-permute-start.3 = (f32[4,24,64]{2,0,1:T(4,128)S(1)}, f32[4,24,64]{2,0,1:T(4,128)S(1)}, u32[]{:S(2)}, u32[]{:S(2)}) collective-permute-start(f32[4,24,64]{2,0,1:T(4,128)S(1)} %pad_maximum_fusion.3), channel_id=1, source_target_pairs={{4,0},{8,4},{12,8},{16,12},{20,16},{24,20},{28,24},{32,28},{36,32}... | collective-permute-start | bytes 73736 | tf_op jit(solution)/shard_map/ppermute | solution.py:19
  70.2 8.2 %collective-permute-start.23 = (f32[64]{0:T(128)S(1)}, f32[64]{0:T(128)S(1)}, u32[]{:S(2)}, u32[]{:S(2)}) collective-permute-start(f32[64]{0:T(128)S(1)} %convolution_bitcast_fusion.14), channel_id=1, source_target_pairs={{32,0},{36,4},{40,8},{44,12},{48,16},{52,20},{56,24},{60,28},{64,3... | collective-permute-start | bytes 776 | tf_op jit(solution)/shard_map/ppermute | solution.py:27
  78.4 233.1 %collective-permute-start = (f32[4,24,512]{2,0,1:T(4,128)S(1)}, f32[4,24,512]{2,0,1:T(4,128)S(1)}, u32[]{:S(2)}, u32[]{:S(2)}) collective-permute-start(f32[4,24,512]{2,0,1:T(4,128)S(1)} %all_gather.3), channel_id=1, source_target_pairs={{0,4},{4,8},{8,12},{12,16},{16,20},{20,24},{24,28},{28,32},{32,36}... | collective-permute-start | bytes 589832 | tf_op jit(solution)/shard_map/ppermute | solution.py:18
  83.2 228.3 %collective-permute-start.1 = (f32[4,24,512]{2,0,1:T(4,128)S(1)}, f32[4,24,512]{2,0,1:T(4,128)S(1)}, u32[]{:S(2)}, u32[]{:S(2)}) collective-permute-start(f32[4,24,512]{2,0,1:T(4,128)S(1)} %all_gather.3), channel_id=1, source_target_pairs={{4,0},{8,4},{12,8},{16,12},{20,16},{24,20},{28,24},{32,28},{36,32}... | collective-permute-start | bytes 589832 | tf_op jit(solution)/shard_map/ppermute | solution.py:19
  85.3 7.8 %collective-permute-start.12 = (f32[4,64]{1,0:T(4,128)S(1)}, f32[4,64]{1,0:T(4,128)S(1)}, u32[]{:S(2)}, u32[]{:S(2)}) collective-permute-start(f32[4,64]{1,0:T(4,128)S(1)} %pad_maximum_fusion.5), channel_id=1, source_target_pairs={{24,0},{28,4},{32,8},{36,12},{40,16},{44,20},{48,24},{52,28},{56,3... | collective-permute-start | bytes 3080 | tf_op jit(solution)/shard_map/ppermute | solution.py:27
  93.1 6.2 %collective-permute-start.11 = (f32[4,64]{1,0:T(4,128)S(1)}, f32[4,64]{1,0:T(4,128)S(1)}, u32[]{:S(2)}, u32[]{:S(2)}) collective-permute-start(f32[4,64]{1,0:T(4,128)S(1)} %pad_maximum_fusion.5), channel_id=1, source_target_pairs={{16,0},{20,4},{24,8},{28,12},{32,16},{36,20},{40,24},{44,28},{48,3... | collective-permute-start | bytes 3080 | tf_op jit(solution)/shard_map/ppermute | solution.py:27
  99.4 6.2 %collective-permute-start.10 = (f32[4,64]{1,0:T(4,128)S(1)}, f32[4,64]{1,0:T(4,128)S(1)}, u32[]{:S(2)}, u32[]{:S(2)}) collective-permute-start(f32[4,64]{1,0:T(4,128)S(1)} %pad_maximum_fusion.5), channel_id=1, source_target_pairs={{0,16},{4,20},{8,24},{12,28},{16,32},{20,36},{24,40},{28,44},{32,4... | collective-permute-start | bytes 3080 | tf_op jit(solution)/shard_map/ppermute | solution.py:27
  105.6 9.3 %collective-permute-start.28 = (f32[64]{0:T(128)S(1)}, f32[64]{0:T(128)S(1)}, u32[]{:S(2)}, u32[]{:S(2)}) collective-permute-start(f32[64]{0:T(128)S(1)} %convolution_bitcast_fusion.9), channel_id=1, source_target_pairs={{64,0},{68,4},{72,8},{76,12},{80,16},{84,20},{88,24},{92,28},{96,3... | collective-permute-start | bytes 776 | tf_op jit(solution)/shard_map/ppermute | solution.py:27
  114.9 2.0 collective-permute-start.9
  116.9 11.4 %collective-permute-start.17 = (f32[4,64]{1,0:T(4,128)S(1)}, f32[4,64]{1,0:T(4,128)S(1)}, u32[]{:S(2)}, u32[]{:S(2)}) collective-permute-start(f32[4,64]{1,0:T(4,128)S(1)} %pad_maximum_fusion.6), channel_id=1, source_target_pairs={{48,0},{52,4},{56,8},{60,12},{64,16},{68,20},{72,24},{76,28},{80,3... | collective-permute-start | bytes 3080 | tf_op jit(solution)/shard_map/ppermute | solution.py:27
  128.3 8.2 %collective-permute-start.16 = (f32[4,64]{1,0:T(4,128)S(1)}, f32[4,64]{1,0:T(4,128)S(1)}, u32[]{:S(2)}, u32[]{:S(2)}) collective-permute-start(f32[4,64]{1,0:T(4,128)S(1)} %pad_maximum_fusion.6), channel_id=1, source_target_pairs={{32,0},{36,4},{40,8},{44,12},{48,16},{52,20},{56,24},{60,28},{64,3... | collective-permute-start | bytes 3080 | tf_op jit(solution)/shard_map/ppermute | solution.py:27
  136.5 7.5 %collective-permute-start.15 = (f32[4,64]{1,0:T(4,128)S(1)}, f32[4,64]{1,0:T(4,128)S(1)}, u32[]{:S(2)}, u32[]{:S(2)}) collective-permute-start(f32[4,64]{1,0:T(4,128)S(1)} %pad_maximum_fusion.6), channel_id=1, source_target_pairs={{0,32},{4,36},{8,40},{12,44},{16,48},{20,52},{24,56},{28,60},{32,6... | collective-permute-start | bytes 3080 | tf_op jit(solution)/shard_map/ppermute | solution.py:27
  144.0 8.5 %collective-permute-start.14 = (f32[4,64]{1,0:T(4,128)S(1)}, f32[4,64]{1,0:T(4,128)S(1)}, u32[]{:S(2)}, u32[]{:S(2)}) collective-permute-start(f32[4,64]{1,0:T(4,128)S(1)} %pad_maximum_fusion.6), channel_id=1, source_target_pairs={{0,48},{4,52},{8,56},{12,60},{16,64},{20,68},{24,72},{28,76},{32,8... | collective-permute-start | bytes 3080 | tf_op jit(solution)/shard_map/ppermute | solution.py:27
  152.5 15.9 %collective-permute-start.22 = (f32[4,64]{1,0:T(4,128)S(1)}, f32[4,64]{1,0:T(4,128)S(1)}, u32[]{:S(2)}, u32[]{:S(2)}) collective-permute-start(f32[4,64]{1,0:T(4,128)S(1)} %pad_maximum_fusion.7), channel_id=1, source_target_pairs={{96,0},{100,4},{104,8},{108,12},{112,16},{116,20},{120,24},{124,28... | collective-permute-start | bytes 3080 | tf_op jit(solution)/shard_map/ppermute | solution.py:27
  168.3 5.3 collective-permute-start.20
  173.6 6.7 %collective-permute-start.21 = (f32[4,64]{1,0:T(4,128)S(1)}, f32[4,64]{1,0:T(4,128)S(1)}, u32[]{:S(2)}, u32[]{:S(2)}) collective-permute-start(f32[4,64]{1,0:T(4,128)S(1)} %pad_maximum_fusion.7), channel_id=1, source_target_pairs={{64,0},{68,4},{72,8},{76,12},{80,16},{84,20},{88,24},{92,28},{96,3... | collective-permute-start | bytes 3080 | tf_op jit(solution)/shard_map/ppermute | solution.py:27
  180.3 11.0 %collective-permute-start.19 = (f32[4,64]{1,0:T(4,128)S(1)}, f32[4,64]{1,0:T(4,128)S(1)}, u32[]{:S(2)}, u32[]{:S(2)}) collective-permute-start(f32[4,64]{1,0:T(4,128)S(1)} %pad_maximum_fusion.7), channel_id=1, source_target_pairs={{0,96},{4,100},{8,104},{12,108},{16,112},{20,116},{24,120},{28,124... | collective-permute-start | bytes 3080 | tf_op jit(solution)/shard_map/ppermute | solution.py:27
  191.3 8.6 %collective-permute-start.25 = (f32[4,64]{1,0:T(4,128)S(1)}, f32[4,64]{1,0:T(4,128)S(1)}, u32[]{:S(2)}, u32[]{:S(2)}) collective-permute-start(f32[4,64]{1,0:T(4,128)S(1)} %pad_maximum_fusion.8), channel_id=1, source_target_pairs={{0,128},{4,132},{8,136},{12,140},{16,144},{20,148},{24,152},{28,15... | collective-permute-start | bytes 3080 | tf_op jit(solution)/shard_map/ppermute | solution.py:27
  199.9 8.2 %collective-permute-start.26 = (f32[4,64]{1,0:T(4,128)S(1)}, f32[4,64]{1,0:T(4,128)S(1)}, u32[]{:S(2)}, u32[]{:S(2)}) collective-permute-start(f32[4,64]{1,0:T(4,128)S(1)} %pad_maximum_fusion.8), channel_id=1, source_target_pairs={{128,0},{132,4},{136,8},{140,12},{144,16},{148,20},{152,24},{156,2... | collective-permute-start | bytes 3080 | tf_op jit(solution)/shard_map/ppermute | solution.py:27
  208.1 6.5 %collective-permute-start.27 = (f32[4,64]{1,0:T(4,128)S(1)}, f32[4,64]{1,0:T(4,128)S(1)}, u32[]{:S(2)}, u32[]{:S(2)}) collective-permute-start(f32[4,64]{1,0:T(4,128)S(1)} %pad_maximum_fusion.8), channel_id=1, source_target_pairs={{192,0},{196,4},{200,8},{204,12},{208,16},{212,20},{216,24},{220,2... | collective-permute-start | bytes 3080 | tf_op jit(solution)/shard_map/ppermute | solution.py:27
  214.6 7.1 %collective-permute-start.24 = (f32[4,64]{1,0:T(4,128)S(1)}, f32[4,64]{1,0:T(4,128)S(1)}, u32[]{:S(2)}, u32[]{:S(2)}) collective-permute-start(f32[4,64]{1,0:T(4,128)S(1)} %pad_maximum_fusion.8), channel_id=1, source_target_pairs={{0,192},{4,196},{8,200},{12,204},{16,208},{20,212},{24,216},{28,22... | collective-permute-start | bytes 3080 | tf_op jit(solution)/shard_map/ppermute | solution.py:27
  221.7 8.6 %collective-permute-start.30 = (f32[4,64]{1,0:T(4,128)S(1)}, f32[4,64]{1,0:T(4,128)S(1)}, u32[]{:S(2)}, u32[]{:S(2)}) collective-permute-start(f32[4,64]{1,0:T(4,128)S(1)} %pad_maximum_fusion.9), channel_id=1, source_target_pairs={{0,256},{4,260},{8,264},{12,268},{16,272},{20,276},{24,280},{28,28... | collective-permute-start | bytes 3080 | tf_op jit(solution)/shard_map/ppermute | solution.py:27
  230.3 8.3 %collective-permute-start.31 = (f32[4,64]{1,0:T(4,128)S(1)}, f32[4,64]{1,0:T(4,128)S(1)}, u32[]{:S(2)}, u32[]{:S(2)}) collective-permute-start(f32[4,64]{1,0:T(4,128)S(1)} %pad_maximum_fusion.9), channel_id=1, source_target_pairs={{256,0},{260,4},{264,8},{268,12},{272,16},{276,20},{280,24},{284,2... | collective-permute-start | bytes 3080 | tf_op jit(solution)/shard_map/ppermute | solution.py:27
  238.5 6.4 %collective-permute-start.32 = (f32[4,64]{1,0:T(4,128)S(1)}, f32[4,64]{1,0:T(4,128)S(1)}, u32[]{:S(2)}, u32[]{:S(2)}) collective-permute-start(f32[4,64]{1,0:T(4,128)S(1)} %pad_maximum_fusion.9), channel_id=1, source_target_pairs={{384,0},{388,4},{392,8},{396,12},{400,16},{404,20},{408,24},{412,2... | collective-permute-start | bytes 3080 | tf_op jit(solution)/shard_map/ppermute | solution.py:27
  244.9 2.4 collective-permute-start.29
  248.4 2.0 collective-permute-start.33
  250.5 3.3 collective-permute-start.34
  254.0 4.9 collective-permute-start.35
  259.0 2.0 collective-permute-start.36
  261.1 32.1 %collective-permute-start.37 = (f32[64]{0:T(128)S(1)}, f32[64]{0:T(128)S(1)}, u32[]{:S(2)}, u32[]{:S(2)}) collective-permute-start(f32[64]{0:T(128)S(1)} %fusion.27), channel_id=1, source_target_pairs={{0,4},{4,8},{8,12},{12,16},{16,20},{20,24},{24,28},{28,32},{32,36}... | collective-permute-start | bytes 776 | tf_op jit(solution)/shard_map/ppermute | solution.py:27
  311.7 88.0 %copy-start.3 = (f32[24,128]{1,0:T(8,128)S(1)}, f32[24,128]{1,0:T(8,128)}, u32[]{:S(2)}) copy-start(f32[24,128]{1,0:T(8,128)} %param.23) | copy-start | bytes 36868
  311.7 88.0 %copy-start.7 = (f32[24,128]{1,0:T(8,128)S(1)}, f32[24,128]{1,0:T(8,128)}, u32[]{:S(2)}) copy-start(f32[24,128]{1,0:T(8,128)} %param.20) | copy-start | bytes 36868
  311.7 88.0 %copy-start.8 = (f32[24,128]{1,0:T(8,128)S(1)}, f32[24,128]{1,0:T(8,128)}, u32[]{:S(2)}) copy-start(f32[24,128]{1,0:T(8,128)} %param.22) | copy-start | bytes 36868
  399.7 115.1 %copy-start.10 = (f32[24,128]{1,0:T(8,128)S(1)}, f32[24,128]{1,0:T(8,128)}, u32[]{:S(2)}) copy-start(f32[24,128]{1,0:T(8,128)} %param.21) | copy-start | bytes 36868
  516.0 97.3 %copy-start.6 = (f32[24,128]{1,0:T(8,128)}, f32[24,128]{1,0:T(8,128)S(1)}, u32[]{:S(2)}) copy-start(f32[24,128]{1,0:T(8,128)S(1)} %get-tuple-element.84) | copy-start | bytes 36868
where the time goes:
time: 615 us; the launch traced here: 613 us
  blocking collectives  243 us (40%)
  starting transfers between devices  154 us (25%)
  waiting for transfers between devices  99.8 us (16%)
  other arithmetic  59.2 us (10%)
  local copies, waits for them, and re-layouts  35.3 us (6%)
  matrix products  15.1 us (2%)
    ppermute x34, starting transfers between devices, passed_along(): return lax.ppermute(shard, axis, pairs)  138 us
    psum x1, blocking collectives, per_device(): lax.psum(jnp.sum(masked_residual * masked_residual), ('leaf', 'near'))  113 us
    ppermute x34, waiting for transfers between devices, passed_along(): return lax.ppermute(shard, axis, pairs)  99.8 us
    psum x1, blocking collectives, per_device(): norm_new = lax.psum(jnp.sum(new_residual * new_residual), ('leaf', 'near'))  95.2 us
    reduce_sum x18, other arithmetic, one_group(): running = running + jnp.sum(kernel_tile * weights[:, None, :], axis=2)  42.1 us
    gather x54, local copies, waits for them, and re-layouts, one_group(): sources = jnp.take(window, jnp.maximum(indices, 0), axis=1)  31.2 us
    psum x1, blocking collectives, per_device(): lax.psum(jnp.einsum('srp,sp->sr', leaf_basis, masked_direction, precision...  14 us
  transfers between devices with their start and end apart: 38, of which 27 were waited for; matrix products, arithmetic and copies ran while one was open for 2% of the time, Pallas kernels for 0%

commit v1 on v0

v1 whole, which is shorter than its diff:
```python
import functools

import jax
import jax.numpy as jnp
from jax import lax
from jax.experimental import pallas as pl
from jax.experimental.pallas import tpu as pltpu
from jax.sharding import PartitionSpec as P

AMPLITUDE = 0.02
SCALE = 2.0 * 1.4426950408889634
HIGHEST = lax.Precision.HIGHEST
MESH = pl.DeviceIdType.MESH
F32 = jnp.float32
BF16 = jnp.bfloat16
CAP = 24
NEAR = 4
PLANE = 16
PLANES = 8
NEAR_NB = 9
LEVELS = 6
SPLIT_ROWS = 48
TINY = 1e-12


def pieces(tile):
    high = tile.astype(BF16).astype(F32)
    rest = tile - high
    middle = rest.astype(BF16).astype(F32)
    return high, middle, rest - middle


def decay(squared):
    clamped = jnp.maximum(squared, TINY)
    return jnp.exp2(-(clamped * lax.rsqrt(clamped)))


def row_times(row, matrix, transposed):
    dims = (((1,), (1 if transposed else 0,)), ((), ()))
    wide = jnp.broadcast_to(row, (8, row.shape[1]))
    return lax.dot_general(
        wide, matrix, dims, precision=HIGHEST, preferred_element_type=F32
    )[0:1]


def padded_square(block):
    rows, lanes = block.shape
    if lanes < 128:
        block = jnp.concatenate([block, jnp.zeros((rows, 128 - lanes), F32)], axis=1)
    if rows < 128:
        block = jnp.concatenate([block, jnp.zeros((128 - rows, 128), F32)], axis=0)
    return block


def kernel(
    count_ref, near_ref, far_ref,
    pos_ref, noise_ref, sol_ref, res_ref, dir_ref, basis_ref, lskel_ref, ltrans_ref,
    btrans_ref, bskel_ref,
    new_sol_ref, new_res_ref, new_dir_ref,
    win0, win1, win2, win3, split0, split3, wb0, wb3, tsplit, products0, products3, acc, near_rows,
    cbuf, fbuf, farwin, ftarget, pbuf, bufa, big, small, far_rows, ebuf, far_vals, targets,
    hop1, hop2, hop3,
    win_s, win_r, c_s, c_r, l_s, l_r, p_s, p_r, relay_s, relay_r, a_s, a_r, b_s, b_r, g_s, g_r,
    f_s, f_r, h1_s, h1_r, h2_s, h2_r, h3_s, h3_r,
):
    leaf = lax.axis_index("leaf")
    near = lax.axis_index("near")
    plane = leaf // PLANE
    place = lax.rem(leaf, PLANE)
    across = place // 2
    core = lax.rem(place, 2)
    wins = (win0, win1, win2, win3)

    def to(leaf_at, near_at):
        return {"leaf": leaf_at, "near": near_at}

    def send_to(src, dst, send_sem, recv_sem, leaf_at, near_at):
        return pltpu.make_async_remote_copy(
            src_ref=src, dst_ref=dst, send_sem=send_sem, recv_sem=recv_sem,
            device_id=to(leaf_at, near_at), device_id_type=MESH,
        )

    def near_at(step):
        return lax.rem(near + step, NEAR)

    def leaf_at(step):
        return lax.rem(leaf + step + PLANE * PLANES, PLANE * PLANES)

    def plane_peer(step):
        return plane * PLANE + lax.rem(place + step, PLANE)

    def depth_peer(step):
        return lax.rem(plane + step + PLANES, PLANES) * PLANE + place

    barrier = pltpu.get_barrier_semaphore()

    def greet(leaf_to, near_to):
        pl.semaphore_signal(barrier, inc=1, device_id=to(leaf_to, near_to), device_id_type=MESH)

    for step in range(1, NEAR):
        greet(leaf, near_at(step))
    for way in (1, -1):
        for step in range(NEAR):
            greet(leaf_at(way), near_at(step))

    @pl.loop(1, PLANE)
    def _(step):
        greet(plane_peer(step), near)

    @pl.loop(1, PLANES)
    def _(step):
        greet(depth_peer(step), near)

    count = count_ref[0]
    occupied = lax.broadcasted_iota(jnp.int32, (CAP, 128), 0) < count
    direction = jnp.where(occupied, dir_ref[...], 0.0)
    for component in range(3):
        win0[pl.ds(96 + component, CAP, stride=4), :] = pos_ref[component] * SCALE
    win0[pl.ds(99, CAP, stride=4), :] = direction

    pl.semaphore_wait(barrier, 3 + 8 + PLANE - 1 + PLANES - 1)

    own = win0.at[pl.ds(96, 96), :]
    window_copies = {}
    number = 0
    for way, group in ((1, 0), (-1, 2), (0, 1)):
        for step in range(NEAR):
            if way == 0 and step == 0:
                continue
            chunk = (NEAR - step) % NEAR
            window_copies[way, step] = send_to(
                own, wins[chunk].at[pl.ds(96 * group, 96), :], win_s.at[number], win_r.at[number],
                leaf_at(way), near_at(step),
            )
            number += 1
    for way in (1, -1):
        window_copies[way, 0].start()

    pair_copies = []
    for level, first in ((2, 0), (3, 1), (4, 4)):
        span = 2 ** (level - 1)
        for step in range(1, span):
            pair_copies.append((span, send_to(
                btrans_ref.at[0, level], pbuf.at[level - 1], p_s.at[first + step - 1], p_r.at[level - 2],
                leaf_at(2 * step), near,
            )))
    relay = send_to(pbuf, pbuf, relay_s, relay_r, leaf_at(1), near)

    @pl.when(core == 0)
    def _():
        pbuf[0] = btrans_ref[0, 1]
        for level in (2, 3, 4):
            @pl.when(lax.rem(across, 2 ** (level - 1)) == 0)
            def _(level=level):
                pbuf[level - 1] = btrans_ref[0, level]
                for span, copy in pair_copies:
                    if span == 2 ** (level - 1):
                        copy.start()

    lanes64 = lax.broadcasted_iota(jnp.int32, (64, 128), 1)

    def one_coeff(slot, columns):
        product = basis_ref[slot] * jnp.where(slot < count, dir_ref[pl.ds(slot, 1), :], 0.0)
        return jnp.where(lanes64 == slot, jnp.sum(product, axis=1, keepdims=True), columns)

    columns = lax.fori_loop(0, CAP, one_coeff, jnp.zeros((64, 128), F32), unroll=4)
    cbuf[near] = padded_square(columns).T[0:CAP, 0:64]
    c_copies = []
    for step in range(1, NEAR):
        copy = send_to(cbuf.at[near], cbuf.at[near], c_s.at[step - 1], c_r.at[step - 1], leaf, near_at(step))
        copy.start()
        c_copies.append(copy)
    for way in (0, 1, -1):
        for step in range(1, NEAR):
            window_copies[way, step].start()

    sub = lax.broadcasted_iota(jnp.int32, (8, 128), 0)
    centre = jnp.zeros((8, 128), F32)
    for component in range(3):
        middle = jnp.mean(pos_ref[component]) * SCALE
        centre = jnp.where((sub == component) | (sub == component + 4), middle, centre)

    def extended(tile):
        square = tile * tile
        norm = square[0:1] + square[1:2] + square[2:3]
        return norm

    def prepare_target(pair, carry):
        tile = win0[pl.ds(pl.multiple_of(96 + 8 * pair, 8), 8), :] - centre
        for half in range(2):
            base = tile if half == 0 else pltpu.roll(tile, 4, 0)
            norm = extended(base)
            rows = jnp.where(sub < 3, -2.0 * base, jnp.where(sub == 3, 1.0, jnp.where(sub == 4, norm, 0.0)))
            high, middle, low = pieces(rows)
            stacked = jnp.concatenate(
                [high, high, middle, middle, high, low, jnp.zeros((128 - SPLIT_ROWS, 128), F32)], axis=0
            )
            tsplit[2 * pair + half] = stacked.T[:, 0:SPLIT_ROWS].astype(BF16)
        return carry

    lax.fori_loop(0, CAP // 2, prepare_target, 0)

    def prepare_sources(window, split, weights, at, lanes):
        split[3 * CAP, :, lanes] = jnp.zeros((SPLIT_ROWS, 128), BF16)
        weights[3 * CAP, at] = jnp.zeros((8, 128), F32)

        def one(pair, carry):
            tile = window[pl.ds(pl.multiple_of(8 * pair, 8), 8), :] - centre
            for half in range(2):
                base = tile if half == 0 else pltpu.roll(tile, 4, 0)
                norm = extended(base)
                rows = jnp.where(sub < 3, base, jnp.where(sub == 3, norm, jnp.where(sub == 4, 1.0, 0.0)))
                high, middle, low = pieces(rows)
                stacked = jnp.concatenate([high, middle, high, middle, low, high], axis=0)
                split[2 * pair + half, :, lanes] = stacked.astype(BF16)
                weights[2 * pair + half, at] = jnp.broadcast_to(base[3:4], (8, 128))
            return carry

        lax.fori_loop(0, 3 * CAP // 2, one, 0, unroll=2)

    skeleton_rows = padded_square(
        jnp.concatenate([lskel_ref[0], lskel_ref[1], lskel_ref[2]], axis=0) * SCALE
    ).T
    for row in range(3 * CAP):
        ftarget[row] = jnp.broadcast_to(skeleton_rows[0:64, row:row + 1], (64, 64))
    for component in range(3):
        farwin[component, CAP:2 * CAP, :] = lskel_ref[component] * SCALE
    farwin[:, 3 * CAP:, :] = jnp.zeros((4, 8, 64), F32)

    for copy in c_copies:
        copy.wait_recv()
    coeffs = cbuf[0] + cbuf[1] + cbuf[2] + cbuf[3]
    farwin[3, CAP:2 * CAP, :] = coeffs
    l_copies = []
    for number, (way, group) in enumerate(((1, 0), (-1, 2))):
        copy = send_to(
            farwin.at[:, pl.ds(CAP, CAP), :], farwin.at[:, pl.ds(CAP * group, CAP), :],
            l_s.at[number], l_r.at[number], leaf_at(way), near,
        )
        copy.start()
        l_copies.append(copy)

    for level in (2, 3, 4):
        @pl.when((core == 0) & (lax.rem(across, 2 ** (level - 1)) != 0))
        def _(level=level):
            send_to(
                btrans_ref.at[0, level], pbuf.at[level - 1], p_s.at[0], p_r.at[level - 2], leaf, near
            ).wait_recv()

    @pl.when(core == 0)
    def _():
        relay.start()

    total = jnp.zeros((64, 64), F32)
    for slot in range(CAP):
        total = total + ltrans_ref[slot] * farwin[3, CAP + slot:CAP + slot + 1, :]
    lifted = padded_square(jnp.broadcast_to(jnp.sum(total, axis=1, keepdims=True), (64, 128))).T[0:1, 0:64]

    @pl.when(core == 1)
    def _():
        relay.wait_recv()

    bufa[place] = jnp.zeros((32, 64), F32)
    bufa[place, 0:1, :] = lifted
    for level in range(LEVELS - 1):
        matrix = btrans_ref[0, 0] if level == 0 else pbuf[level - 1]
        lifted = row_times(lifted, matrix, True)
        bufa[place, level + 1:level + 2, :] = lifted
    for component in range(3):
        bufa[place, 8 * (component + 1):8 * (component + 1) + LEVELS, :] = bskel_ref[component, 0] * SCALE

    def a_copy(step):
        return send_to(bufa.at[place], bufa.at[place], a_s.at[step], a_r.at[step], plane_peer(step), near)

    @pl.loop(1, PLANE)
    def _(step):
        a_copy(step).start()

    def near_slots(low, high, split, weights, products, width, first):
        def listed(slot, place_in_list):
            index = near_ref[slot, place_in_list]
            return jnp.where(index < 0, 3 * CAP, index)

        def multiply(slot, index, buffer):
            products[buffer] = jnp.dot(tsplit[slot], split[index], preferred_element_type=F32)

        def one_slot(slot, carry):
            indices = [listed(slot, k) for k in range(NEAR_NB)]
            following = jnp.minimum(slot + 1, CAP - 1)
            if first:
                sums = [jnp.zeros((8, 128), F32)] * 16
            else:
                sums = [acc[slot, 8 * g:8 * g + 8, :] for g in range(16)]
            for k in range(NEAR_NB):
                if k + 1 < NEAR_NB:
                    multiply(slot, indices[k + 1], (k + 1) % 3)
                else:
                    multiply(following, listed(following, 0), 0)
                weight = [weights[indices[k], j] for j in range(width)]
                for g in range(16):
                    for j in range(width):
                        tile = decay(products[k % 3, 8 * g:8 * g + 8, 128 * j:128 * j + 128])
                        sums[g] = sums[g] + tile * weight[j]
            if first:
                for g in range(16):
                    acc[slot, 8 * g:8 * g + 8, :] = sums[g]
            else:
                whole = jnp.concatenate(sums, axis=0).T
                near_rows[pl.ds(slot, 1), :] = jnp.sum(whole, axis=0, keepdims=True)
            return carry

        multiply(low, listed(low, 0), 0)
        lax.fori_loop(low, high, one_slot, 0)

    for way in (1, -1):
        window_copies[way, 0].wait_recv()
    prepare_sources(win0, split0, wb0, 0, slice(0, 128))
    near_slots(0, CAP, split0, wb0, products0, 1, True)

    @pl.loop(1, PLANE)
    def _(step):
        a_copy(step).wait_recv()

    sums = [bufa[i, 0:8, :] for i in range(PLANE)]
    offset = 0
    for level in range(LEVELS):
        span = 2 ** min(level, 4)
        if 0 < level < 5:
            sums = [sums[2 * i] + sums[2 * i + 1] for i in range(len(sums) // 2)]
        for box in range(PLANE // span):
            rows = [sums[box][level:level + 1, :]] + [
                bufa[box * span, 8 * (c + 1) + level:8 * (c + 1) + level + 1, :] for c in range(3)
            ]
            for c in range(4):
                if level < 3:
                    big[1, c, offset + box:offset + box + 1, :] = rows[c]
                else:
                    at = 4 * c + (0, 2, 3)[level - 3] + box
                    small[plane, at:at + 1, :] = rows[c]
        offset += PLANE // span

    def b_copy(step):
        return send_to(small.at[plane], small.at[plane], b_s.at[step], b_r.at[step], depth_peer(step), near)

    @pl.loop(1, PLANES)
    def _(step):
        b_copy(step).start()

    g_copies = []
    for number, (way, slot) in enumerate(((1, 0), (-1, 2))):
        copy = send_to(big.at[1], big.at[slot], g_s.at[number], g_r.at[number], depth_peer(way), near)
        copy.start()
        g_copies.append(copy)

    for way in (1, -1, 0):
        for step in range(1, NEAR):
            window_copies[way, step].wait_recv()
    for j in range(3):
        prepare_sources(wins[j + 1], split3, wb3, j, slice(128 * j, 128 * j + 128))
    near_slots(0, 8, split3, wb3, products3, 3, False)

    for copy in l_copies:
        copy.wait_recv()

    def one_far(slot, carry):
        target = [ftarget[c * CAP + slot] for c in range(3)]
        running = jnp.zeros((64, 64), F32)
        for k in range(2):
            index = far_ref[slot, k]
            index = jnp.where(index < 0, 3 * CAP, index)
            squared = jnp.zeros((64, 64), F32)
            for c in range(3):
                spacing = target[c] - farwin[c, pl.ds(index, 1), :]
                squared = squared + spacing * spacing
            running = running + decay(squared) * farwin[3, pl.ds(index, 1), :]
        return jnp.where(lanes64 == slot, jnp.sum(running, axis=1, keepdims=True), carry)

    far_columns = lax.fori_loop(0, CAP, one_far, jnp.zeros((64, 128), F32), unroll=2)
    fbuf[near] = padded_square(far_columns).T[0:CAP, 0:64] * AMPLITUDE
    f_copies = []
    for step in range(1, NEAR):
        copy = send_to(fbuf.at[near], fbuf.at[near], f_s.at[step - 1], f_r.at[step - 1], leaf, near_at(step))
        copy.start()
        f_copies.append(copy)

    @pl.loop(1, PLANES)
    def _(step):
        b_copy(step).wait_recv()

    for copy in g_copies:
        copy.wait_recv()
    targets[...] = jnp.zeros((128, 128), F32)
    for level in range(LEVELS):
        for c in range(3):
            if level < 5:
                first = place // 2 ** level * 2 ** level
                row = bufa[first, 8 * (c + 1) + level:8 * (c + 1) + level + 1, :]
            else:
                row = small[plane // 2 * 2, 4 * c + 7:4 * c + 8, :]
            targets[3 * level + c:3 * level + c + 1, 0:64] = row
    turned = targets[...].T
    offsets = (0, 16, 24)
    field_columns = jnp.zeros((64, 128), F32)
    for level in range(LEVELS):
        box = leaf // 2 ** level
        boxes = PLANE * PLANES // 2 ** level
        target = [jnp.broadcast_to(turned[0:64, 3 * level + c:3 * level + c + 1], (64, 64)) for c in range(3)]
        running = jnp.zeros((64, 64), F32)
        for away in (jnp.where(lax.rem(box, 2) == 1, -3, 3), -2, 2):
            other = box + away
            exists = (other >= 0) & (other < boxes)
            other = jnp.clip(other, 0, boxes - 1)
            if level < 3:
                each = PLANE // 2 ** level
                other_plane = other // each - plane + 1
                at = offsets[level] + lax.rem(other, each)
                rows = [big[other_plane, c, pl.ds(at, 1), :] for c in range(4)]
            elif level < 5:
                each = PLANE // 2 ** level
                at = (0, 2)[level - 3] + lax.rem(other, each)
                rows = [small[other // each, pl.ds(4 * c + at, 1), :] for c in range(4)]
            else:
                rows = [small[2 * other, 4 * c + 3:4 * c + 4, :] for c in range(4)]
                rows[0] = rows[0] + small[2 * other + 1, 3:4, :]
            squared = jnp.zeros((64, 64), F32)
            for c in range(3):
                spacing = target[c] - rows[c + 1]
                squared = squared + spacing * spacing
            running = running + decay(squared) * jnp.where(exists, rows[0], 0.0)
        field_columns = jnp.where(lanes64 == level, jnp.sum(running, axis=1, keepdims=True), field_columns)
    fields = padded_square(field_columns).T[0:8, 0:64] * AMPLITUDE
    downward = fields[LEVELS - 1:LEVELS]
    for level in range(LEVELS - 2, -1, -1):
        matrix = btrans_ref[0, 0] if level == 0 else pbuf[level - 1]
        downward = fields[level:level + 1] + row_times(downward, matrix, False)
    down_column = jnp.broadcast_to(
        jnp.concatenate([downward, jnp.zeros((1, 64), F32)], axis=1), (128, 128)
    ).T[0:64, 0:64]
    for slot in range(CAP):
        far_rows[slot:slot + 1, :] = jnp.sum(ltrans_ref[slot] * down_column, axis=0, keepdims=True)

    near_slots(8, 16, split3, wb3, products3, 3, False)

    for copy in f_copies:
        copy.wait_recv()
    expansion = far_rows[...] + (fbuf[0] + fbuf[1] + fbuf[2] + fbuf[3])
    expansion_columns = padded_square(expansion).T
    for slot in range(CAP):
        far_vals[slot:slot + 1, :] = jnp.sum(
            basis_ref[slot] * expansion_columns[0:64, slot:slot + 1], axis=0, keepdims=True
        )

    near_slots(16, CAP, split3, wb3, products3, 3, False)

    residual = jnp.where(occupied, res_ref[...], 0.0)
    image = jnp.where(
        occupied, noise_ref[...] * direction + AMPLITUDE * near_rows[...] + far_vals[...], 0.0
    )
    tile = jnp.zeros((8, 128), F32)
    for number, product in enumerate(
        (residual * residual, direction * image, residual * image, image * image)
    ):
        tile = jnp.where(sub == number, jnp.sum(product, axis=0, keepdims=True), tile)

    hop1[near] = tile
    h1_copies = []
    for step in range(1, NEAR):
        copy = send_to(hop1.at[near], hop1.at[near], h1_s.at[step], h1_r.at[step], leaf, near_at(step))
        copy.start()
        h1_copies.append(copy)
    for copy in h1_copies:
        copy.wait_recv()
    tile = hop1[0] + hop1[1] + hop1[2] + hop1[3]

    hop2[place] = tile

    def h2_copy(step):
        return send_to(hop2.at[place], hop2.at[place], h2_s.at[step], h2_r.at[step], plane_peer(step), near)

    @pl.loop(1, PLANE)
    def _(step):
        h2_copy(step).start()

    @pl.loop(1, PLANE)
    def _(step):
        h2_copy(step).wait_recv()

    tile = jnp.sum(hop2[...], axis=0)

    hop3[plane] = tile

    def h3_copy(step):
        return send_to(hop3.at[plane], hop3.at[plane], h3_s.at[step], h3_r.at[step], depth_peer(step), near)

    @pl.loop(1, PLANES)
    def _(step):
        h3_copy(step).start()

    @pl.loop(1, PLANES)
    def _(step):
        h3_copy(step).wait_recv()

    totals = jnp.sum(jnp.sum(hop3[...], axis=0), axis=1, keepdims=True)
    norm_old, curvature, mixed, image_norm = (totals[i:i + 1] for i in range(4))
    step_length = norm_old / curvature
    norm_new = norm_old - 2.0 * step_length * mixed + step_length * step_length * image_norm
    new_residual = residual - step_length * image
    new_sol_ref[...] = jnp.where(occupied, sol_ref[...], 0.0) + step_length * direction
    new_res_ref[...] = new_residual
    new_dir_ref[...] = new_residual + norm_new / norm_old * direction

    for copy in window_copies.values():
        copy.wait_send()

    @pl.when(core == 0)
    def _():
        relay.wait_send()
        for level in (2, 3, 4):
            @pl.when(lax.rem(across, 2 ** (level - 1)) == 0)
            def _(level=level):
                for span, copy in pair_copies:
                    if span == 2 ** (level - 1):
                        copy.wait_send()

    for copy in c_copies + l_copies + g_copies + f_copies + h1_copies:
        copy.wait_send()

    @pl.loop(1, PLANE)
    def _(step):
        a_copy(step).wait_send()
        h2_copy(step).wait_send()

    @pl.loop(1, PLANES)
    def _(step):
        b_copy(step).wait_send()
        h3_copy(step).wait_send()


def per_device(
    positions, noise_variance, solution, residual, direction, leaf_basis, leaf_skeleton,
    leaf_transfer, box_transfer, box_skeleton, leaf_count, near_list, far_list,
):
    vmem = pl.BlockSpec(memory_space=pltpu.VMEM)
    smem = pl.BlockSpec(memory_space=pltpu.SMEM)
    dma = pltpu.SemaphoreType.DMA
    out = jax.ShapeDtypeStruct((CAP, 128), F32)
    slots = 3 * CAP + 1
    return pl.pallas_call(
        kernel,
        out_shape=(out, out, out),
        in_specs=[smem] * 3 + [vmem] * 10,
        out_specs=(vmem, vmem, vmem),
        scratch_shapes=[
            *[pltpu.VMEM((12 * CAP, 128), F32)] * 4,
            pltpu.VMEM((slots, SPLIT_ROWS, 128), BF16),
            pltpu.VMEM((slots, SPLIT_ROWS, 384), BF16),
            pltpu.VMEM((slots, 1, 8, 128), F32),
            pltpu.VMEM((slots, 3, 8, 128), F32),
            pltpu.VMEM((CAP, 128, SPLIT_ROWS), BF16),
            pltpu.VMEM((3, 128, 128), F32),
            pltpu.VMEM((3, 128, 384), F32),
            pltpu.VMEM((CAP, 128, 128), F32),
            pltpu.VMEM((CAP, 128), F32),
            pltpu.VMEM((NEAR, CAP, 64), F32),
            pltpu.VMEM((NEAR, CAP, 64), F32),
            pltpu.VMEM((4, 3 * CAP + 8, 64), F32),
            pltpu.VMEM((3 * CAP, 64, 64), F32),
            pltpu.VMEM((4, 64, 64), F32),
            pltpu.VMEM((PLANE, 32, 64), F32),
            pltpu.VMEM((3, 4, 32, 64), F32),
            pltpu.VMEM((PLANES, 16, 64), F32),
            pltpu.VMEM((CAP, 64), F32),
            pltpu.VMEM((CAP, 64), F32),
            pltpu.VMEM((CAP, 128), F32),
            pltpu.VMEM((128, 128), F32),
            pltpu.VMEM((NEAR, 8, 128), F32),
            pltpu.VMEM((PLANE, 8, 128), F32),
            pltpu.VMEM((PLANES, 8, 128), F32),
            dma((11,)), dma((11,)), dma((3,)), dma((3,)), dma((2,)), dma((2,)),
            dma((11,)), dma((3,)), dma, dma, dma((PLANE,)), dma((PLANE,)),
            dma((PLANES,)), dma((PLANES,)), dma((2,)), dma((2,)),
            dma((3,)), dma((3,)), dma((NEAR,)), dma((NEAR,)),
            dma((PLANE,)), dma((PLANE,)), dma((PLANES,)), dma((PLANES,)),
        ],
        compiler_params=pltpu.CompilerParams(
            collective_id=0, has_side_effects=True, vmem_limit_bytes=48 * 2**20
        ),
        name="iteration",
    )(
        leaf_count, near_list, far_list,
        positions, noise_variance, solution, residual, direction, leaf_basis, leaf_skeleton,
        leaf_transfer, box_transfer, box_skeleton,
    )


def solution(mesh):
    return jax.shard_map(
        per_device,
        mesh=mesh,
        in_specs=(
            P(None, "leaf", "near"),
            P("leaf", "near"),
            P("leaf", "near"),
            P("leaf", "near"),
            P("leaf", "near"),
            P("leaf", None, "near"),
            P(None, "leaf", None),
            P("leaf", None, None),
            P("leaf", None, None, None),
            P(None, "leaf", None, None),
            P("leaf"),
            P("leaf", None),
            P("leaf", "near"),
        ),
        out_specs=(P("leaf", "near"), P("leaf", "near"), P("leaf", "near")),
        check_vma=False,
    )
```

time: 615 us -> 82.2 us (0.13)
  blocking collectives: 243 us -> 0 us
  starting transfers between devices: 154 us -> 0 us
  waiting for transfers between devices: 99.8 us -> 0 us
  Pallas kernels: 0 us -> 70.8 us
  other arithmetic: 59.2 us -> 0 us
  local copies, waits for them, and re-layouts: 35.3 us -> 9.46 us
  matrix products: 15.1 us -> 0 us
    psum x4 -> x0, blocking collectives: 233 us -> none  [the longest x1 113 us: per_device(): lax.psum(jnp.sum(masked_residual * masked_residual), ('leaf', 'near'))]
    ppermute x38 -> x0, starting transfers between devices: 154 us -> none  [the longest x34 138 us: passed_along(): return lax.ppermute(shard, axis, pairs)]
    ppermute x38 -> x0, waiting for transfers between devices: 99.8 us -> none  [the longest x34 99.8 us: passed_along(): return lax.ppermute(shard, axis, pairs)]
    pallas_call x0 -> x1, Pallas kernels: none -> 70.8 us  [per_device(): pl.pallas_call(kernel, out_shape=(out, out, out), in_specs=[smem] * 3 + [...]
    reduce_sum x20 -> x0, other arithmetic: 44 us -> none  [the longest x18 42.1 us: one_group(): running = running + jnp.sum(kernel_tile * weights[:, None, :], axis=2)]
    gather x56 -> x0, local copies, waits for them, and re-layouts: 32.4 us -> none  [the longest x54 31.2 us: one_group(): sources = jnp.take(window, jnp.maximum(indices, 0), axis=1)]
    dot_general x40 -> x0, matrix products: 15.1 us -> none  [the longest x24 6.23 us: per_device(): contribution = jnp.dot(kernel_tile, incoming[3], precision=HIGHEST)]
    all_gather x1 -> x0, blocking collectives: 10.1 us -> none  [per_device(): whole_leaves = lax.all_gather(packed, 'near', axis=2, tiled=True)]
  transfers between devices with their start and end apart: 38 -> 0, of which waited for: 27 -> 0; matrix products, arithmetic and copies ran while one was open for 2% -> 0% of each run, Pallas kernels for 0% -> 0%
where the time goes in v1:
time: 82.2 us; the launch traced here: 81.6 us
  Pallas kernels  70.8 us (86%)
  local copies, waits for them, and re-layouts  9.46 us (12%)
  between operations  1.32 us (2%)
    pallas_call x1, Pallas kernels, per_device(): pl.pallas_call(kernel, out_shape=(out, out, out), in_specs=[smem] * 3 + [...  70.8 us
    unnamed x26, local copies, waits for them, and re-layouts  9.46 us

profile of v1, /device:TPU:1, one launch (start us, length us, event | category | flops | bytes accessed | tf_op | source)
XLA Modules:
  0.0 81.6 jit_solution(5674344257291941034)
XLA Ops:
  0.6 0.0 copy-start.3
  1.3 0.0 copy-start.9
  1.3 0.7 copy.18.bskel_ref
  2.0 0.0 copy-start.5
  2.0 0.8 copy.16.near_ref
  2.8 0.0 copy-done.9
  2.8 0.1 copy.17.far_ref
  2.9 0.0 copy-done.3
  2.9 0.0 copy-done.5
  2.9 0.0 copy-start
  2.9 1.1 %copy-done = f32[24,64,128]{2,1,0:T(8,128)S(1)} copy-done((f32[24,64,128]{2,1,0:T(8,128)S(1)}, f32[24,64,128]{2,1,0:T(8,128)}, u32[]{:S(2)}) %copy-start) | copy-done | bytes 786456
  4.0 0.0 copy-start.1
  4.0 1.1 %copy-done.1 = f32[24,64,64]{2,1,0:T(8,128)S(1)} copy-done((f32[24,64,64]{2,1,0:T(8,128)S(1)}, f32[24,64,64]{2,1,0:T(8,128)}, u32[]{:S(2)}) %copy-start.1) | copy-done | bytes 393240
  5.2 0.0 copy-start.2
  5.2 0.9 %copy-done.2 = f32[1,5,64,64]{3,2,1,0:T(8,128)S(1)} copy-done((f32[1,5,64,64]{3,2,1,0:T(8,128)S(1)}, f32[1,5,64,64]{3,2,1,0:T(8,128)}, u32[]{:S(2)}) %copy-start.2) | copy-done | bytes 81944
  6.1 0.0 copy-start.4
  6.1 0.8 copy-done.4
  6.8 0.0 copy-start.6
  6.8 0.7 copy-done.6
  7.6 0.0 copy-start.7
  7.6 0.7 copy-done.7
  8.3 0.0 copy-start.8
  8.3 0.7 copy-done.8
  9.0 70.8 %iteration.1 = (f32[24,128]{1,0:T(8,128)S(1)}, f32[24,128]{1,0:T(8,128)S(1)}, f32[24,128]{1,0:T(8,128)S(1)}) custom-call(s32[1]{0:T(128)S(6)} %copy.22.count_ref, s32[24,9]{1,0:T(8,128)S(1)} %copy.16.near_ref, s32[24,2]{1,0:T(8,128)S(1)} %copy.17.far_ref, f32[3,24,128]{2,1,0:T(8,128)S(1)} %copy-done.3, f32[24,128]{1,0:T(8,128)S(1)} %copy-done.5, ...), custom_call_target="tpu_custom_call" | custom-call | tf_op jit(solution)/shard_map/iteration/pallas_call | solution.py:548
  79.8 0.6 copy.23
  80.4 0.6 copy.24
  81.0 0.6 copy.25
Async XLA Ops:
  0.6 2.3 %copy-start.3 = (f32[3,24,128]{2,1,0:T(8,128)S(1)}, f32[3,24,128]{2,1,0:T(8,128)}, u32[]{:S(2)}) copy-start(f32[3,24,128]{2,1,0:T(8,128)} %pos_ref.1) | copy-start | bytes 110596
  1.3 1.5 %copy-start.9 = (s32[24,2]{0,1:T(2,128)S(1)}, s32[24,2]{0,1:T(2,128)}, u32[]{:S(2)}) copy-start(s32[24,2]{0,1:T(2,128)} %param.25) | copy-start | bytes 580
  2.0 0.9 %copy-start.5 = (f32[24,128]{1,0:T(8,128)S(1)}, f32[24,128]{1,0:T(8,128)}, u32[]{:S(2)}) copy-start(f32[24,128]{1,0:T(8,128)} %noise_ref.1) | copy-start | bytes 36868
  2.9 1.1 %copy-start = (f32[24,64,128]{2,1,0:T(8,128)S(1)}, f32[24,64,128]{2,1,0:T(8,128)}, u32[]{:S(2)}) copy-start(f32[24,64,128]{2,1,0:T(8,128)} %basis_ref.1) | copy-start | bytes 2359300
  4.0 1.1 %copy-start.1 = (f32[24,64,64]{2,1,0:T(8,128)S(1)}, f32[24,64,64]{2,1,0:T(8,128)}, u32[]{:S(2)}) copy-start(f32[24,64,64]{2,1,0:T(8,128)} %ltrans_ref.1) | copy-start | bytes 1179652
  5.2 0.9 %copy-start.2 = (f32[1,5,64,64]{3,2,1,0:T(8,128)S(1)}, f32[1,5,64,64]{3,2,1,0:T(8,128)}, u32[]{:S(2)}) copy-start(f32[1,5,64,64]{3,2,1,0:T(8,128)} %btrans_ref.1) | copy-start | bytes 245764
  6.1 0.8 copy-start.4
  6.8 0.7 copy-start.6
  7.6 0.7 copy-start.7
  8.3 0.7 copy-start.8

commit v2 on v1

--- a/solution.py
+++ b/solution.py
@@ -54,14 +54,14 @@
 
 def kernel(
     count_ref, near_ref, far_ref,
-    pos_ref, noise_ref, sol_ref, res_ref, dir_ref, basis_ref, lskel_ref, ltrans_ref,
-    btrans_ref, bskel_ref,
-    new_sol_ref, new_res_ref, new_dir_ref,
-    win0, win1, win2, win3, split0, split3, wb0, wb3, tsplit, products0, products3, acc, near_rows,
-    cbuf, fbuf, farwin, ftarget, pbuf, bufa, big, small, far_rows, ebuf, far_vals, targets,
-    hop1, hop2, hop3,
+    pos_in, noise_in, sol_in, res_in, dir_in, basis_in, lskel_in, ltrans_in, btrans_in, bskel_in,
+    kept_sol_ref, kept_res_ref, res_step_ref, kept_dir_ref, step_ref, ratio_ref,
+    pos_ref, noise_ref, sol_ref, res_ref, dir_ref, basis_ref, lskel_ref, ltrans_ref, btrans_ref, bskel_ref, in_sem,
+    win0, win1, win2, win3, split0, split3, wb0, wb3, tsplit, products, acc, near_rows,
+    cbuf, fbuf, farwin, ftarget, psend, pbuf, bufa, big, small, far_rows, ebuf, far_vals, targets,
+    hop1, hop2,
     win_s, win_r, c_s, c_r, l_s, l_r, p_s, p_r, relay_s, relay_r, a_s, a_r, b_s, b_r, g_s, g_r,
-    f_s, f_r, h1_s, h1_r, h2_s, h2_r, h3_s, h3_r,
+    f_s, f_r, h1_s, h1_r, h2_s, h2_r,
 ):
     leaf = lax.axis_index("leaf")
     near = lax.axis_index("near")
@@ -92,13 +92,21 @@
     def depth_peer(step):
         return lax.rem(plane + step + PLANES, PLANES) * PLANE + place
 
+    loads = {}
+    for number, (name, src, dst) in enumerate((
+        ("pos", pos_in, pos_ref), ("dir", dir_in, dir_ref), ("basis", basis_in, basis_ref),
+        ("btrans", btrans_in, btrans_ref), ("lskel", lskel_in, lskel_ref), ("ltrans", ltrans_in, ltrans_ref),
+        ("bskel", bskel_in, bskel_ref), ("noise", noise_in, noise_ref), ("res", res_in, res_ref),
+        ("sol", sol_in, sol_ref),
+    )):
+        loads[name] = pltpu.make_async_copy(src, dst, in_sem.at[number])
+        loads[name].start()
+
     barrier = pltpu.get_barrier_semaphore()
 
     def greet(leaf_to, near_to):
         pl.semaphore_signal(barrier, inc=1, device_id=to(leaf_to, near_to), device_id_type=MESH)
 
-    for step in range(1, NEAR):
-        greet(leaf, near_at(step))
     for way in (1, -1):
         for step in range(NEAR):
             greet(leaf_at(way), near_at(step))
@@ -107,18 +115,20 @@
     def _(step):
         greet(plane_peer(step), near)
 
-    @pl.loop(1, PLANES)
-    def _(step):
-        greet(depth_peer(step), near)
+    @pl.loop(1, PLANES * NEAR)
+    def _(step):
+        greet(depth_peer(step // NEAR), near_at(lax.rem(step, NEAR)))
 
     count = count_ref[0]
+    loads["pos"].wait()
+    loads["dir"].wait()
     occupied = lax.broadcasted_iota(jnp.int32, (CAP, 128), 0) < count
     direction = jnp.where(occupied, dir_ref[...], 0.0)
     for component in range(3):
         win0[pl.ds(96 + component, CAP, stride=4), :] = pos_ref[component] * SCALE
     win0[pl.ds(99, CAP, stride=4), :] = direction
 
-    pl.semaphore_wait(barrier, 3 + 8 + PLANE - 1 + PLANES - 1)
+    pl.semaphore_wait(barrier, 8 + PLANE - 1 + PLANES * NEAR - 1)
 
     own = win0.at[pl.ds(96, 96), :]
     window_copies = {}
@@ -136,27 +146,39 @@
     for way in (1, -1):
         window_copies[way, 0].start()
 
+    loads["btrans"].wait()
+    def packed(matrix):
+        return jnp.concatenate([matrix[0:32], matrix[32:64]], axis=1)
+
+    def ancestor(level):
+        if level == 0:
+            return btrans_ref[0, 0]
+        both = pbuf[level - 1]
+        return jnp.concatenate([both[:, 0:64], both[:, 64:128]], axis=0)
+
     pair_copies = []
     for level, first in ((2, 0), (3, 1), (4, 4)):
         span = 2 ** (level - 1)
         for step in range(1, span):
             pair_copies.append((span, send_to(
-                btrans_ref.at[0, level], pbuf.at[level - 1], p_s.at[first + step - 1], p_r.at[level - 2],
+                psend.at[level - 1], pbuf.at[level - 1], p_s.at[first + step - 1], p_r.at[level - 2],
                 leaf_at(2 * step), near,
             )))
     relay = send_to(pbuf, pbuf, relay_s, relay_r, leaf_at(1), near)
 
     @pl.when(core == 0)
     def _():
-        pbuf[0] = btrans_ref[0, 1]
+        pbuf[0] = packed(btrans_ref[0, 1])
         for level in (2, 3, 4):
             @pl.when(lax.rem(across, 2 ** (level - 1)) == 0)
             def _(level=level):
-                pbuf[level - 1] = btrans_ref[0, level]
+                psend[level - 1] = packed(btrans_ref[0, level])
+                pbuf[level - 1] = psend[level - 1]
                 for span, copy in pair_copies:
                     if span == 2 ** (level - 1):
                         copy.start()
 
+    loads["basis"].wait()
     lanes64 = lax.broadcasted_iota(jnp.int32, (64, 128), 1)
 
     def one_coeff(slot, columns):
@@ -218,6 +240,8 @@
 
         lax.fori_loop(0, 3 * CAP // 2, one, 0, unroll=2)
 
+    for name in ("lskel", "ltrans", "bskel", "noise", "res", "sol"):
+        loads[name].wait()
     skeleton_rows = padded_square(
         jnp.concatenate([lskel_ref[0], lskel_ref[1], lskel_ref[2]], axis=0) * SCALE
     ).T
@@ -244,7 +268,7 @@
         @pl.when((core == 0) & (lax.rem(across, 2 ** (level - 1)) != 0))
         def _(level=level):
             send_to(
-                btrans_ref.at[0, level], pbuf.at[level - 1], p_s.at[0], p_r.at[level - 2], leaf, near
+                psend.at[level - 1], pbuf.at[level - 1], p_s.at[0], p_r.at[level - 2], leaf, near
             ).wait_recv()
 
     @pl.when(core == 0)
@@ -260,14 +284,13 @@
     def _():
         relay.wait_recv()
 
-    bufa[place] = jnp.zeros((32, 64), F32)
-    bufa[place, 0:1, :] = lifted
+    bufa[place] = jnp.zeros((16, 128), F32)
+    bufa[place, 0:1, 0:64] = lifted
     for level in range(LEVELS - 1):
-        matrix = btrans_ref[0, 0] if level == 0 else pbuf[level - 1]
-        lifted = row_times(lifted, matrix, True)
-        bufa[place, level + 1:level + 2, :] = lifted
-    for component in range(3):
-        bufa[place, 8 * (component + 1):8 * (component + 1) + LEVELS, :] = bskel_ref[component, 0] * SCALE
+        lifted = row_times(lifted, ancestor(level), True)
+        bufa[place, level + 1:level + 2, 0:64] = lifted
+    for component, (row, lane) in enumerate(((0, 64), (8, 0), (8, 64))):
+        bufa[place, row:row + LEVELS, lane:lane + 64] = bskel_ref[component, :, 0, :] * SCALE
 
     def a_copy(step):
         return send_to(bufa.at[place], bufa.at[place], a_s.at[step], a_r.at[step], plane_peer(step), near)
@@ -276,51 +299,64 @@
     def _(step):
         a_copy(step).start()
 
-    def near_slots(low, high, split, weights, products, width, first):
-        def listed(slot, place_in_list):
-            index = near_ref[slot, place_in_list]
+    def near_slots(low, high, split, weights, width, first, slots):
+        chunks = [(k, j) for k in range(NEAR_NB) for j in range(width)]
+        units = [chunks[i:i + 2] for i in range(0, len(chunks), 2)]
+
+        def listed(slot, k):
+            index = near_ref[k, slot]
             return jnp.where(index < 0, 3 * CAP, index)
 
-        def multiply(slot, index, buffer):
-            products[buffer] = jnp.dot(tsplit[slot], split[index], preferred_element_type=F32)
-
-        def one_slot(slot, carry):
-            indices = [listed(slot, k) for k in range(NEAR_NB)]
-            following = jnp.minimum(slot + 1, CAP - 1)
-            if first:
-                sums = [jnp.zeros((8, 128), F32)] * 16
-            else:
-                sums = [acc[slot, 8 * g:8 * g + 8, :] for g in range(16)]
-            for k in range(NEAR_NB):
-                if k + 1 < NEAR_NB:
-                    multiply(slot, indices[k + 1], (k + 1) % 3)
-                else:
-                    multiply(following, listed(following, 0), 0)
-                weight = [weights[indices[k], j] for j in range(width)]
+        def buffer_of(u):
+            return 0 if u == 0 else 1 + (u - 1) % 2
+
+        def multiply(slot, u):
+            parts = [split[listed(slot, k), :, 128 * j:128 * j + 128] for k, j in units[u]]
+            sources = jnp.concatenate(parts, axis=1) if len(parts) > 1 else parts[0]
+            products[buffer_of(u), :, 0:128 * len(parts)] = jnp.dot(
+                tsplit[slot], sources, preferred_element_type=F32
+            )
+
+        def some_slots(step, carry):
+            start = low + step * slots
+            work = [(start + i, u) for i in range(slots) for u in range(len(units))]
+            following = jnp.minimum(start + slots, CAP - 1)
+            sums = []
+            for at, (slot, u) in enumerate(work):
+                if u == 0:
+                    if first:
+                        sums = [jnp.zeros((8, 128), F32)] * 16
+                    else:
+                        sums = [acc[slot, 8 * g:8 * g + 8, :] for g in range(16)]
+                next_slot, next_u = work[at + 1] if at + 1 < len(work) else (following, 0)
+                multiply(next_slot, next_u)
+                weight = [weights[listed(slot, k), j] for k, j in units[u]]
                 for g in range(16):
-                    for j in range(width):
-                        tile = decay(products[k % 3, 8 * g:8 * g + 8, 128 * j:128 * j + 128])
-                        sums[g] = sums[g] + tile * weight[j]
-            if first:
-                for g in range(16):
-                    acc[slot, 8 * g:8 * g + 8, :] = sums[g]
-            else:
-                whole = jnp.concatenate(sums, axis=0).T
-                near_rows[pl.ds(slot, 1), :] = jnp.sum(whole, axis=0, keepdims=True)
+                    for i in range(len(weight)):
+                        tile = decay(products[buffer_of(u), 8 * g:8 * g + 8, 128 * i:128 * i + 128])
+                        sums[g] = sums[g] + tile * weight[i]
+                if u + 1 == len(units):
+                    if first:
+                        for g in range(16):
+                            acc[slot, 8 * g:8 * g + 8, :] = sums[g]
+                    else:
+                        whole = jnp.concatenate(sums, axis=0).T
+                        near_rows[pl.ds(slot, 1), :] = jnp.sum(whole, axis=0, keepdims=True)
             return carry
 
-        multiply(low, listed(low, 0), 0)
-        lax.fori_loop(low, high, one_slot, 0)
+        multiply(low, 0)
+        lax.fori_loop(0, (high - low) // slots, some_slots, 0)
 
     for way in (1, -1):
         window_copies[way, 0].wait_recv()
     prepare_sources(win0, split0, wb0, 0, slice(0, 128))
-    near_slots(0, CAP, split0, wb0, products0, 1, True)
+    near_slots(0, CAP, split0, wb0, 1, True, 4)
 
     @pl.loop(1, PLANE)
     def _(step):
         a_copy(step).wait_recv()
 
+    low_lanes = lax.broadcasted_iota(jnp.int32, (1, 128), 1) < 64
     sums = [bufa[i, 0:8, :] for i in range(PLANE)]
     offset = 0
     for level in range(LEVELS):
@@ -328,15 +364,17 @@
         if 0 < level < 5:
             sums = [sums[2 * i] + sums[2 * i + 1] for i in range(len(sums) // 2)]
         for box in range(PLANE // span):
-            rows = [sums[box][level:level + 1, :]] + [
-                bufa[box * span, 8 * (c + 1) + level:8 * (c + 1) + level + 1, :] for c in range(3)
-            ]
-            for c in range(4):
+            own = bufa[box * span]
+            rows = (
+                jnp.where(low_lanes, sums[box][level:level + 1], own[level:level + 1]),
+                own[8 + level:9 + level],
+            )
+            for half in range(2):
                 if level < 3:
-                    big[1, c, offset + box:offset + box + 1, :] = rows[c]
+                    big[1, half, offset + box:offset + box + 1, :] = rows[half]
                 else:
-                    at = 4 * c + (0, 2, 3)[level - 3] + box
-                    small[plane, at:at + 1, :] = rows[c]
+                    at = 4 * half + (0, 2, 3)[level - 3] + box
+                    small[plane, at:at + 1, :] = rows[half]
         offset += PLANE // span
 
     def b_copy(step):
@@ -357,7 +395,7 @@
             window_copies[way, step].wait_recv()
     for j in range(3):
         prepare_sources(wins[j + 1], split3, wb3, j, slice(128 * j, 128 * j + 128))
-    near_slots(0, 8, split3, wb3, products3, 3, False)
+    near_slots(0, 8, split3, wb3, 3, False, 2)
 
     for copy in l_copies:
         copy.wait_recv()
@@ -366,7 +404,7 @@
         target = [ftarget[c * CAP + slot] for c in range(3)]
         running = jnp.zeros((64, 64), F32)
         for k in range(2):
-            index = far_ref[slot, k]
+            index = far_ref[k, slot]
             index = jnp.where(index < 0, 3 * CAP, index)
             squared = jnp.zeros((64, 64), F32)
             for c in range(3):
@@ -375,7 +413,7 @@
             running = running + decay(squared) * farwin[3, pl.ds(index, 1), :]
         return jnp.where(lanes64 == slot, jnp.sum(running, axis=1, keepdims=True), carry)
 
-    far_columns = lax.fori_loop(0, CAP, one_far, jnp.zeros((64, 128), F32), unroll=2)
+    far_columns = lax.fori_loop(0, CAP, one_far, jnp.zeros((64, 128), F32), unroll=6)
     fbuf[near] = padded_square(far_columns).T[0:CAP, 0:64] * AMPLITUDE
     f_copies = []
     for step in range(1, NEAR):
@@ -391,20 +429,23 @@
         copy.wait_recv()
     targets[...] = jnp.zeros((128, 128), F32)
     for level in range(LEVELS):
-        for c in range(3):
+        first = place // 2 ** level * 2 ** level
+        for half in range(2):
             if level < 5:
-                first = place // 2 ** level * 2 ** level
-                row = bufa[first, 8 * (c + 1) + level:8 * (c + 1) + level + 1, :]
+                row = bufa[first, 8 * half + level:8 * half + level + 1, :]
             else:
-                row = small[plane // 2 * 2, 4 * c + 7:4 * c + 8, :]
-            targets[3 * level + c:3 * level + c + 1, 0:64] = row
+                row = small[plane // 2 * 2, 4 * half + 3:4 * half + 4, :]
+            targets[2 * level + half:2 * level + half + 1, :] = row
     turned = targets[...].T
     offsets = (0, 16, 24)
     field_columns = jnp.zeros((64, 128), F32)
     for level in range(LEVELS):
         box = leaf // 2 ** level
         boxes = PLANE * PLANES // 2 ** level
-        target = [jnp.broadcast_to(turned[0:64, 3 * level + c:3 * level + c + 1], (64, 64)) for c in range(3)]
+        target = [
+            jnp.broadcast_to(turned[lane:lane + 64, 2 * level + half:2 * level + half + 1], (64, 64))
+            for half, lane in ((0, 64), (1, 0), (1, 64))
+        ]
         running = jnp.zeros((64, 64), F32)
         for away in (jnp.where(lax.rem(box, 2) == 1, -3, 3), -2, 2):
             other = box + away
@@ -414,14 +455,15 @@
                 each = PLANE // 2 ** level
                 other_plane = other // each - plane + 1
                 at = offsets[level] + lax.rem(other, each)
-                rows = [big[other_plane, c, pl.ds(at, 1), :] for c in range(4)]
+                halves = [big[other_plane, half, pl.ds(at, 1), :] for half in range(2)]
             elif level < 5:
                 each = PLANE // 2 ** level
                 at = (0, 2)[level - 3] + lax.rem(other, each)
-                rows = [small[other // each, pl.ds(4 * c + at, 1), :] for c in range(4)]
+                halves = [small[other // each, pl.ds(4 * half + at, 1), :] for half in range(2)]
             else:
-                rows = [small[2 * other, 4 * c + 3:4 * c + 4, :] for c in range(4)]
-                rows[0] = rows[0] + small[2 * other + 1, 3:4, :]
+                halves = [small[2 * other, 4 * half + 3:4 * half + 4, :] for half in range(2)]
+                halves[0] = halves[0] + jnp.where(low_lanes, small[2 * other + 1, 3:4, :], 0.0)
+            rows = [half[:, lane:lane + 64] for half in halves for lane in (0, 64)]
             squared = jnp.zeros((64, 64), F32)
             for c in range(3):
                 spacing = target[c] - rows[c + 1]
@@ -431,15 +473,14 @@
     fields = padded_square(field_columns).T[0:8, 0:64] * AMPLITUDE
     downward = fields[LEVELS - 1:LEVELS]
     for level in range(LEVELS - 2, -1, -1):
-        matrix = btrans_ref[0, 0] if level == 0 else pbuf[level - 1]
-        downward = fields[level:level + 1] + row_times(downward, matrix, False)
+        downward = fields[level:level + 1] + row_times(downward, ancestor(level), False)
     down_column = jnp.broadcast_to(
         jnp.concatenate([downward, jnp.zeros((1, 64), F32)], axis=1), (128, 128)
     ).T[0:64, 0:64]
     for slot in range(CAP):
         far_rows[slot:slot + 1, :] = jnp.sum(ltrans_ref[slot] * down_column, axis=0, keepdims=True)
 
-    near_slots(8, 16, split3, wb3, products3, 3, False)
+    near_slots(8, 16, split3, wb3, 3, False, 2)
 
     for copy in f_copies:
         copy.wait_recv()
@@ -450,64 +491,58 @@
             basis_ref[slot] * expansion_columns[0:64, slot:slot + 1], axis=0, keepdims=True
         )
 
-    near_slots(16, CAP, split3, wb3, products3, 3, False)
+    near_slots(16, CAP, split3, wb3, 3, False, 2)
 
     residual = jnp.where(occupied, res_ref[...], 0.0)
     image = jnp.where(
         occupied, noise_ref[...] * direction + AMPLITUDE * near_rows[...] + far_vals[...], 0.0
     )
+    kept_sol_ref[...] = jnp.where(occupied, sol_ref[...], 0.0)
+    kept_res_ref[...] = residual
     tile = jnp.zeros((8, 128), F32)
     for number, product in enumerate(
         (residual * residual, direction * image, residual * image, image * image)
     ):
         tile = jnp.where(sub == number, jnp.sum(product, axis=0, keepdims=True), tile)
 
-    hop1[near] = tile
-    h1_copies = []
-    for step in range(1, NEAR):
-        copy = send_to(hop1.at[near], hop1.at[near], h1_s.at[step], h1_r.at[step], leaf, near_at(step))
+    lane_group = lax.broadcasted_iota(jnp.int32, (8, 128), 1) // 32
+    tile = tile + pltpu.roll(tile, 64, 1)
+    tile = tile + pltpu.roll(tile, 32, 1)
+    row = jnp.sum(jnp.where(sub == lane_group, tile, 0.0), axis=0, keepdims=True)
+
+    mine = plane * NEAR + near
+    hop1[mine] = row
+    hop_copies = []
+    for depth in range(PLANES):
+        for step in range(NEAR):
+            if depth or step:
+                at = depth * NEAR + step
+                copy = send_to(
+                    hop1.at[mine], hop1.at[mine], h1_s.at[at], h1_r.at[at], depth_peer(depth), near_at(step)
+                )
+                copy.start()
+                hop_copies.append(copy)
+    for copy in hop_copies:
+        copy.wait_recv()
+    hop2[place] = jnp.sum(hop1[...], axis=0)
+    last_copies = []
+    for step in range(1, PLANE):
+        copy = send_to(
+            hop2.at[place], hop2.at[place], h2_s.at[step], h2_r.at[step], plane_peer(step), near
+        )
         copy.start()
-        h1_copies.append(copy)
-    for copy in h1_copies:
+        last_copies.append(copy)
+    for copy in last_copies:
         copy.wait_recv()
-    tile = hop1[0] + hop1[1] + hop1[2] + hop1[3]
-
-    hop2[place] = tile
-
-    def h2_copy(step):
-        return send_to(hop2.at[place], hop2.at[place], h2_s.at[step], h2_r.at[step], plane_peer(step), near)
-
-    @pl.loop(1, PLANE)
-    def _(step):
-        h2_copy(step).start()
-
-    @pl.loop(1, PLANE)
-    def _(step):
-        h2_copy(step).wait_recv()
-
-    tile = jnp.sum(hop2[...], axis=0)
-
-    hop3[plane] = tile
-
-    def h3_copy(step):
-        return send_to(hop3.at[plane], hop3.at[plane], h3_s.at[step], h3_r.at[step], depth_peer(step), near)
-
-    @pl.loop(1, PLANES)
-    def _(step):
-        h3_copy(step).start()
-
-    @pl.loop(1, PLANES)
-    def _(step):
-        h3_copy(step).wait_recv()
-
-    totals = jnp.sum(jnp.sum(hop3[...], axis=0), axis=1, keepdims=True)
+    row = jnp.sum(hop2[...], axis=0)
+    totals = jnp.sum(jnp.where(sub == lane_group, row, 0.0), axis=1, keepdims=True)
     norm_old, curvature, mixed, image_norm = (totals[i:i + 1] for i in range(4))
     step_length = norm_old / curvature
     norm_new = norm_old - 2.0 * step_length * mixed + step_length * step_length * image_norm
-    new_residual = residual - step_length * image
-    new_sol_ref[...] = jnp.where(occupied, sol_ref[...], 0.0) + step_length * direction
-    new_res_ref[...] = new_residual
-    new_dir_ref[...] = new_residual + norm_new / norm_old * direction
+    step_ref[...] = jnp.broadcast_to(step_length, (CAP, 128))
+    res_step_ref[...] = step_length * image
+    ratio_ref[...] = jnp.broadcast_to(norm_new / norm_old, (CAP, 128))
+    kept_dir_ref[...] = direction
 
     for copy in window_copies.values():
         copy.wait_send()
@@ -522,18 +557,16 @@
                     if span == 2 ** (level - 1):
                         copy.wait_send()
 
-    for copy in c_copies + l_copies + g_copies + f_copies + h1_copies:
+    for copy in c_copies + l_copies + g_copies + f_copies + hop_copies + last_copies:
         copy.wait_send()
 
     @pl.loop(1, PLANE)
     def _(step):
         a_copy(step).wait_send()
-        h2_copy(step).wait_send()
 
     @pl.loop(1, PLANES)
     def _(step):
         b_copy(step).wait_send()
-        h3_copy(step).wait_send()
 
 
 def per_device(
@@ -542,55 +575,58 @@
 ):
     vmem = pl.BlockSpec(memory_space=pltpu.VMEM)
     smem = pl.BlockSpec(memory_space=pltpu.SMEM)
+    hbm = pl.BlockSpec(memory_space=pltpu.HBM)
     dma = pltpu.SemaphoreType.DMA
-    out = jax.ShapeDtypeStruct((CAP, 128), F32)
     slots = 3 * CAP + 1
-    return pl.pallas_call(
+    arrays = (
+        positions, noise_variance, solution, residual, direction, leaf_basis, leaf_skeleton,
+        leaf_transfer, box_transfer, box_skeleton.transpose(0, 2, 1, 3),
+    )
+    kept_solution, kept_residual, residual_step, kept_direction, step, ratio = pl.pallas_call(
         kernel,
-        out_shape=(out, out, out),
-        in_specs=[smem] * 3 + [vmem] * 10,
-        out_specs=(vmem, vmem, vmem),
+        out_shape=(jax.ShapeDtypeStruct((CAP, 128), F32),) * 6,
+        in_specs=[smem] * 3 + [hbm] * len(arrays),
+        out_specs=(vmem,) * 6,
         scratch_shapes=[
+            *[pltpu.VMEM(array.shape, F32) for array in arrays],
+            dma((len(arrays),)),
             *[pltpu.VMEM((12 * CAP, 128), F32)] * 4,
             pltpu.VMEM((slots, SPLIT_ROWS, 128), BF16),
             pltpu.VMEM((slots, SPLIT_ROWS, 384), BF16),
             pltpu.VMEM((slots, 1, 8, 128), F32),
             pltpu.VMEM((slots, 3, 8, 128), F32),
             pltpu.VMEM((CAP, 128, SPLIT_ROWS), BF16),
-            pltpu.VMEM((3, 128, 128), F32),
-            pltpu.VMEM((3, 128, 384), F32),
+            pltpu.VMEM((3, 128, 256), F32),
             pltpu.VMEM((CAP, 128, 128), F32),
             pltpu.VMEM((CAP, 128), F32),
             pltpu.VMEM((NEAR, CAP, 64), F32),
             pltpu.VMEM((NEAR, CAP, 64), F32),
             pltpu.VMEM((4, 3 * CAP + 8, 64), F32),
             pltpu.VMEM((3 * CAP, 64, 64), F32),
-            pltpu.VMEM((4, 64, 64), F32),
-            pltpu.VMEM((PLANE, 32, 64), F32),
-            pltpu.VMEM((3, 4, 32, 64), F32),
-            pltpu.VMEM((PLANES, 16, 64), F32),
+            pltpu.VMEM((4, 32, 128), F32),
+            pltpu.VMEM((4, 32, 128), F32),
+            pltpu.VMEM((PLANE, 16, 128), F32),
+            pltpu.VMEM((3, 2, 32, 128), F32),
+            pltpu.VMEM((PLANES, 8, 128), F32),
             pltpu.VMEM((CAP, 64), F32),
             pltpu.VMEM((CAP, 64), F32),
             pltpu.VMEM((CAP, 128), F32),
             pltpu.VMEM((128, 128), F32),
-            pltpu.VMEM((NEAR, 8, 128), F32),
-            pltpu.VMEM((PLANE, 8, 128), F32),
-            pltpu.VMEM((PLANES, 8, 128), F32),
+            pltpu.VMEM((NEAR * PLANES, 1, 128), F32),
+            pltpu.VMEM((PLANE, 1, 128), F32),
             dma((11,)), dma((11,)), dma((3,)), dma((3,)), dma((2,)), dma((2,)),
             dma((11,)), dma((3,)), dma, dma, dma((PLANE,)), dma((PLANE,)),
             dma((PLANES,)), dma((PLANES,)), dma((2,)), dma((2,)),
-            dma((3,)), dma((3,)), dma((NEAR,)), dma((NEAR,)),
-            dma((PLANE,)), dma((PLANE,)), dma((PLANES,)), dma((PLANES,)),
+            dma((3,)), dma((3,)), dma((NEAR * PLANES,)), dma((NEAR * PLANES,)),
+            dma((PLANE,)), dma((PLANE,)),
         ],
         compiler_params=pltpu.CompilerParams(
-            collective_id=0, has_side_effects=True, vmem_limit_bytes=48 * 2**20
+            collective_id=0, has_side_effects=True, vmem_limit_bytes=64 * 2**20
         ),
         name="iteration",
-    )(
-        leaf_count, near_list, far_list,
-        positions, noise_variance, solution, residual, direction, leaf_basis, leaf_skeleton,
-        leaf_transfer, box_transfer, box_skeleton,
-    )
+    )(leaf_count, near_list.T, far_list.T, *arrays)
+    new_residual = kept_residual - residual_step
+    return kept_solution + step * kept_direction, new_residual, new_residual + ratio * kept_direction
 
 
 def solution(mesh):

time: 82.2 us -> 66.6 us (0.81)
  local copies, waits for them, and re-layouts: 9.46 us -> 0 us
  Pallas kernels: 70.8 us -> 63.6 us
  other arithmetic: 0 us -> 1.41 us
    unnamed x26 -> x0, local copies, waits for them, and re-layouts: 9.46 us -> none
    pallas_call x1, Pallas kernels: 70.8 us -> 63.6 us  [per_device(): pl.pallas_call(kernel, out_shape=(jax.ShapeDtypeStruct((CAP, 128), F32),)...]
    add x0 -> x1, other arithmetic: none -> 1.41 us  [per_device(): new_residual + ratio * kept_direction]
where the time goes in v2:
time: 66.6 us; the launch traced here: 66.3 us
  Pallas kernels  63.6 us (95%)
  other arithmetic  1.41 us (2%)
  between operations  1.29 us (2%)
    pallas_call x1, Pallas kernels, per_device(): pl.pallas_call(kernel, out_shape=(jax.ShapeDtypeStruct((CAP, 128), F32),)...  63.6 us
    add x1, other arithmetic, per_device(): new_residual + ratio * kept_direction  1.41 us

profile of v2, /device:TPU:1, one launch (start us, length us, event | category | flops | bytes accessed | tf_op | source)
XLA Modules:
  0.0 66.3 jit_solution(11648340990768790998)
XLA Ops:
  1.3 63.6 %iteration.1 = (f32[24,128]{1,0:T(8,128)}, f32[24,128]{1,0:T(8,128)}, f32[24,128]{1,0:T(8,128)}, f32[24,128]{1,0:T(8,128)}, f32[24,128]{1,0:T(8,128)}, /*index=5*/f32[24,128]{1,0:T(8,128)}) custom-call(s32[1]{0:T(128)S(6)} %copy.16.count_ref, s32[9,24]{1,0:T(8,128)} %bitcast.4, s32[2,24]{1,0:T(2,128)} %bitcast.5, f32[3,24,128]{2,1,0:T(8,128)} %pos_in.1, ...), custom_call_target="tpu_custom_call" | custom-call | tf_op jit(solution)/shard_map/iteration/pallas_call | solution.py:585
  64.9 1.4 %multiply_add_fusion = (f32[24,128]{1,0:T(8,128)}, f32[24,128]{1,0:T(8,128)}, f32[24,128]{1,0:T(8,128)}) fusion(f32[24,128]{1,0:T(8,128)} %get-tuple-element.14, f32[24,128]{1,0:T(8,128)} %get-tuple-element.11, f32[24,128]{1,0:T(8,128)} %get-tuple-element.12, f32[24,128]{1,0:T(8,128)} %get-tuple-element.13, f32[24,128]{1,0:T(8,128)} %get-tuple-element.9, ...), kind=kLoop, calls=%fused_computation | loop fusion | flops 15360 | bytes 110592 | tf_op jit(solution)/shard_map/add | solution.py:629

commit v3 on v2

--- a/solution.py
+++ b/solution.py
@@ -92,6 +92,23 @@
     def depth_peer(step):
         return lax.rem(plane + step + PLANES, PLANES) * PLANE + place
 
+    barrier = pltpu.get_barrier_semaphore()
+
+    def greet(leaf_to, near_to):
+        pl.semaphore_signal(barrier, inc=1, device_id=to(leaf_to, near_to), device_id_type=MESH)
+
+    for way in (1, -1):
+        for step in range(NEAR):
+            greet(leaf_at(way), near_at(step))
+
+    @pl.loop(1, PLANE)
+    def _(step):
+        greet(plane_peer(step), near)
+
+    @pl.loop(1, PLANES * NEAR)
+    def _(step):
+        greet(depth_peer(step // NEAR), near_at(lax.rem(step, NEAR)))
+
     loads = {}
     for number, (name, src, dst) in enumerate((
         ("pos", pos_in, pos_ref), ("dir", dir_in, dir_ref), ("basis", basis_in, basis_ref),
@@ -101,23 +118,6 @@
     )):
         loads[name] = pltpu.make_async_copy(src, dst, in_sem.at[number])
         loads[name].start()
-
-    barrier = pltpu.get_barrier_semaphore()
-
-    def greet(leaf_to, near_to):
-        pl.semaphore_signal(barrier, inc=1, device_id=to(leaf_to, near_to), device_id_type=MESH)
-
-    for way in (1, -1):
-        for step in range(NEAR):
-            greet(leaf_at(way), near_at(step))
-
-    @pl.loop(1, PLANE)
-    def _(step):
-        greet(plane_peer(step), near)
-
-    @pl.loop(1, PLANES * NEAR)
-    def _(step):
-        greet(depth_peer(step // NEAR), near_at(lax.rem(step, NEAR)))
 
     count = count_ref[0]
     loads["pos"].wait()
@@ -251,55 +251,7 @@
         farwin[component, CAP:2 * CAP, :] = lskel_ref[component] * SCALE
     farwin[:, 3 * CAP:, :] = jnp.zeros((4, 8, 64), F32)
 
-    for copy in c_copies:
-        copy.wait_recv()
-    coeffs = cbuf[0] + cbuf[1] + cbuf[2] + cbuf[3]
-    farwin[3, CAP:2 * CAP, :] = coeffs
-    l_copies = []
-    for number, (way, group) in enumerate(((1, 0), (-1, 2))):
-        copy = send_to(
-            farwin.at[:, pl.ds(CAP, CAP), :], farwin.at[:, pl.ds(CAP * group, CAP), :],
-            l_s.at[number], l_r.at[number], leaf_at(way), near,
-        )
-        copy.start()
-        l_copies.append(copy)
-
-    for level in (2, 3, 4):
-        @pl.when((core == 0) & (lax.rem(across, 2 ** (level - 1)) != 0))
-        def _(level=level):
-            send_to(
-                psend.at[level - 1], pbuf.at[level - 1], p_s.at[0], p_r.at[level - 2], leaf, near
-            ).wait_recv()
-
-    @pl.when(core == 0)
-    def _():
-        relay.start()
-
-    total = jnp.zeros((64, 64), F32)
-    for slot in range(CAP):
-        total = total + ltrans_ref[slot] * farwin[3, CAP + slot:CAP + slot + 1, :]
-    lifted = padded_square(jnp.broadcast_to(jnp.sum(total, axis=1, keepdims=True), (64, 128))).T[0:1, 0:64]
-
-    @pl.when(core == 1)
-    def _():
-        relay.wait_recv()
-
-    bufa[place] = jnp.zeros((16, 128), F32)
-    bufa[place, 0:1, 0:64] = lifted
-    for level in range(LEVELS - 1):
-        lifted = row_times(lifted, ancestor(level), True)
-        bufa[place, level + 1:level + 2, 0:64] = lifted
-    for component, (row, lane) in enumerate(((0, 64), (8, 0), (8, 64))):
-        bufa[place, row:row + LEVELS, lane:lane + 64] = bskel_ref[component, :, 0, :] * SCALE
-
-    def a_copy(step):
-        return send_to(bufa.at[place], bufa.at[place], a_s.at[step], a_r.at[step], plane_peer(step), near)
-
-    @pl.loop(1, PLANE)
-    def _(step):
-        a_copy(step).start()
-
-    def near_slots(low, high, split, weights, width, first, slots):
+    def near_slots(low, high, split, weights, width, first, slots, inline=False):
         chunks = [(k, j) for k in range(NEAR_NB) for j in range(width)]
         units = [chunks[i:i + 2] for i in range(0, len(chunks), 2)]
 
@@ -345,12 +297,71 @@
             return carry
 
         multiply(low, 0)
-        lax.fori_loop(0, (high - low) // slots, some_slots, 0)
+        if inline:
+            some_slots(0, 0)
+        else:
+            lax.fori_loop(0, (high - low) // slots, some_slots, 0)
 
     for way in (1, -1):
         window_copies[way, 0].wait_recv()
     prepare_sources(win0, split0, wb0, 0, slice(0, 128))
-    near_slots(0, CAP, split0, wb0, 1, True, 4)
+    near_slots(0, 20, split0, wb0, 1, True, 4)
+
+    for level in (2, 3, 4):
+        @pl.when((core == 0) & (lax.rem(across, 2 ** (level - 1)) != 0))
+        def _(level=level):
+            send_to(
+                psend.at[level - 1], pbuf.at[level - 1], p_s.at[0], p_r.at[level - 2], leaf, near
+            ).wait_recv()
+
+    @pl.when(core == 0)
+    def _():
+        relay.start()
+
+    for copy in c_copies:
+        copy.wait_recv()
+    coeffs = cbuf[0] + cbuf[1] + cbuf[2] + cbuf[3]
+    farwin[3, CAP:2 * CAP, :] = coeffs
+    l_copies = []
+    for number, (way, group) in enumerate(((1, 0), (-1, 2))):
+        copy = send_to(
+            farwin.at[:, pl.ds(CAP, CAP), :], farwin.at[:, pl.ds(CAP * group, CAP), :],
+            l_s.at[number], l_r.at[number], leaf_at(way), near,
+        )
+        copy.start()
+        l_copies.append(copy)
+
+    total = jnp.zeros((64, 64), F32)
+    for slot in range(CAP):
+        total = total + ltrans_ref[slot] * farwin[3, CAP + slot:CAP + slot + 1, :]
+    lifted = padded_square(jnp.broadcast_to(jnp.sum(total, axis=1, keepdims=True), (64, 128))).T[0:1, 0:64]
+
+    @pl.when(core == 1)
+    def _():
+        relay.wait_recv()
+
+    near_slots(20, CAP, split0, wb0, 1, True, 4, inline=True)
+    bufa[place] = jnp.zeros((16, 128), F32)
+    bufa[place, 0:1, 0:64] = lifted
+    for level in range(LEVELS - 1):
+        lifted = row_times(lifted, ancestor(level), True)
+        bufa[place, level + 1:level + 2, 0:64] = lifted
+    for component, (row, lane) in enumerate(((0, 64), (8, 0), (8, 64))):
+        bufa[place, row:row + LEVELS, lane:lane + 64] = bskel_ref[component, :, 0, :] * SCALE
+
+    def a_copy(step):
+        return send_to(bufa.at[place], bufa.at[place], a_s.at[step], a_r.at[step], plane_peer(step), near)
+
+    @pl.loop(1, PLANE)
+    def _(step):
+        a_copy(step).start()
+
+    for way in (1, -1, 0):
+        for step in range(1, NEAR):
+            window_copies[way, step].wait_recv()
+    for j in range(3):
+        prepare_sources(wins[j + 1], split3, wb3, j, slice(128 * j, 128 * j + 128))
+    near_slots(0, 10, split3, wb3, 3, False, 2)
 
     @pl.loop(1, PLANE)
     def _(step):
@@ -390,12 +401,7 @@
         copy.start()
         g_copies.append(copy)
 
-    for way in (1, -1, 0):
-        for step in range(1, NEAR):
-            window_copies[way, step].wait_recv()
-    for j in range(3):
-        prepare_sources(wins[j + 1], split3, wb3, j, slice(128 * j, 128 * j + 128))
-    near_slots(0, 8, split3, wb3, 3, False, 2)
+    near_slots(10, 14, split3, wb3, 3, False, 2)
 
     for copy in l_copies:
         copy.wait_recv()
@@ -413,7 +419,10 @@
             running = running + decay(squared) * farwin[3, pl.ds(index, 1), :]
         return jnp.where(lanes64 == slot, jnp.sum(running, axis=1, keepdims=True), carry)
 
-    far_columns = lax.fori_loop(0, CAP, one_far, jnp.zeros((64, 128), F32), unroll=6)
+    near_slots(14, 18, split3, wb3, 3, False, 4, inline=True)
+    far_columns = jnp.zeros((64, 128), F32)
+    for slot in range(CAP):
+        far_columns = one_far(slot, far_columns)
     fbuf[near] = padded_square(far_columns).T[0:CAP, 0:64] * AMPLITUDE
     f_copies = []
     for step in range(1, NEAR):
@@ -427,6 +436,7 @@
 
     for copy in g_copies:
         copy.wait_recv()
+    near_slots(18, 22, split3, wb3, 3, False, 4, inline=True)
     targets[...] = jnp.zeros((128, 128), F32)
     for level in range(LEVELS):
         first = place // 2 ** level * 2 ** level
@@ -480,18 +490,16 @@
     for slot in range(CAP):
         far_rows[slot:slot + 1, :] = jnp.sum(ltrans_ref[slot] * down_column, axis=0, keepdims=True)
 
-    near_slots(8, 16, split3, wb3, 3, False, 2)
 
     for copy in f_copies:
         copy.wait_recv()
+    near_slots(22, CAP, split3, wb3, 3, False, 2, inline=True)
     expansion = far_rows[...] + (fbuf[0] + fbuf[1] + fbuf[2] + fbuf[3])
     expansion_columns = padded_square(expansion).T
     for slot in range(CAP):
         far_vals[slot:slot + 1, :] = jnp.sum(
             basis_ref[slot] * expansion_columns[0:64, slot:slot + 1], axis=0, keepdims=True
         )
-
-    near_slots(16, CAP, split3, wb3, 3, False, 2)
 
     residual = jnp.where(occupied, res_ref[...], 0.0)
     image = jnp.where(

time: 66.6 us -> 62.3 us (0.935)
  Pallas kernels: 63.6 us -> 59.4 us
    pallas_call x1, Pallas kernels: 63.6 us -> 59.4 us  [per_device(): pl.pallas_call(kernel, out_shape=(jax.ShapeDtypeStruct((CAP, 128), F32),)...]
where the time goes in v3:
time: 62.3 us; the launch traced here: 62.1 us
  Pallas kernels  59.4 us (95%)
  other arithmetic  1.41 us (2%)
  between operations  1.29 us (2%)
    pallas_call x1, Pallas kernels, per_device(): pl.pallas_call(kernel, out_shape=(jax.ShapeDtypeStruct((CAP, 128), F32),)...  59.4 us
    add x1, other arithmetic, per_device(): new_residual + ratio * kept_direction  1.41 us

profile of v3, /device:TPU:1, one launch (start us, length us, event | category | flops | bytes accessed | tf_op | source)
XLA Modules:
  0.0 62.1 jit_solution(6777402292016748853)
XLA Ops:
  1.3 59.4 %iteration.1 = (f32[24,128]{1,0:T(8,128)}, f32[24,128]{1,0:T(8,128)}, f32[24,128]{1,0:T(8,128)}, f32[24,128]{1,0:T(8,128)}, f32[24,128]{1,0:T(8,128)}, /*index=5*/f32[24,128]{1,0:T(8,128)}) custom-call(s32[1]{0:T(128)S(6)} %copy.16.count_ref, s32[9,24]{1,0:T(8,128)} %bitcast.4, s32[2,24]{1,0:T(2,128)} %bitcast.5, f32[3,24,128]{2,1,0:T(8,128)} %pos_in.1, ...), custom_call_target="tpu_custom_call" | custom-call | tf_op jit(solution)/shard_map/iteration/pallas_call | solution.py:593
  60.7 1.4 %multiply_add_fusion = (f32[24,128]{1,0:T(8,128)}, f32[24,128]{1,0:T(8,128)}, f32[24,128]{1,0:T(8,128)}) fusion(f32[24,128]{1,0:T(8,128)} %get-tuple-element.14, f32[24,128]{1,0:T(8,128)} %get-tuple-element.11, f32[24,128]{1,0:T(8,128)} %get-tuple-element.12, f32[24,128]{1,0:T(8,128)} %get-tuple-element.13, f32[24,128]{1,0:T(8,128)} %get-tuple-element.9, ...), kind=kLoop, calls=%fused_computation | loop fusion | flops 15360 | bytes 110592 | tf_op jit(solution)/shard_map/add | solution.py:637

commit v4 on v3

--- a/solution.py
+++ b/solution.py
@@ -19,7 +19,7 @@
 PLANES = 8
 NEAR_NB = 9
 LEVELS = 6
-SPLIT_ROWS = 48
+SPLIT_ROWS = 32
 TINY = 1e-12
 
 
@@ -55,7 +55,7 @@
 def kernel(
     count_ref, near_ref, far_ref,
     pos_in, noise_in, sol_in, res_in, dir_in, basis_in, lskel_in, ltrans_in, btrans_in, bskel_in,
-    kept_sol_ref, kept_res_ref, res_step_ref, kept_dir_ref, step_ref, ratio_ref,
+    result_ref,
     pos_ref, noise_ref, sol_ref, res_ref, dir_ref, basis_ref, lskel_ref, ltrans_ref, btrans_ref, bskel_ref, in_sem,
     win0, win1, win2, win3, split0, split3, wb0, wb3, tsplit, products, acc, near_rows,
     cbuf, fbuf, farwin, ftarget, psend, pbuf, bufa, big, small, far_rows, ebuf, far_vals, targets,
@@ -128,7 +128,23 @@
         win0[pl.ds(96 + component, CAP, stride=4), :] = pos_ref[component] * SCALE
     win0[pl.ds(99, CAP, stride=4), :] = direction
 
+    loads["basis"].wait()
+    lanes64 = lax.broadcasted_iota(jnp.int32, (64, 128), 1)
+
+    def one_coeff(slot, columns):
+        product = basis_ref[slot] * jnp.where(slot < count, dir_ref[pl.ds(slot, 1), :], 0.0)
+        return jnp.where(lanes64 == slot, jnp.sum(product, axis=1, keepdims=True), columns)
+
+    columns = lax.fori_loop(0, CAP, one_coeff, jnp.zeros((64, 128), F32), unroll=4)
+    cbuf[near] = padded_square(columns).T[0:CAP, 0:64]
+
     pl.semaphore_wait(barrier, 8 + PLANE - 1 + PLANES * NEAR - 1)
+
+    c_copies = []
+    for step in range(1, NEAR):
+        copy = send_to(cbuf.at[near], cbuf.at[near], c_s.at[step - 1], c_r.at[step - 1], leaf, near_at(step))
+        copy.start()
+        c_copies.append(copy)
 
     own = win0.at[pl.ds(96, 96), :]
     window_copies = {}
@@ -178,20 +194,6 @@
                     if span == 2 ** (level - 1):
                         copy.start()
 
-    loads["basis"].wait()
-    lanes64 = lax.broadcasted_iota(jnp.int32, (64, 128), 1)
-
-    def one_coeff(slot, columns):
-        product = basis_ref[slot] * jnp.where(slot < count, dir_ref[pl.ds(slot, 1), :], 0.0)
-        return jnp.where(lanes64 == slot, jnp.sum(product, axis=1, keepdims=True), columns)
-
-    columns = lax.fori_loop(0, CAP, one_coeff, jnp.zeros((64, 128), F32), unroll=4)
-    cbuf[near] = padded_square(columns).T[0:CAP, 0:64]
-    c_copies = []
-    for step in range(1, NEAR):
-        copy = send_to(cbuf.at[near], cbuf.at[near], c_s.at[step - 1], c_r.at[step - 1], leaf, near_at(step))
-        copy.start()
-        c_copies.append(copy)
     for way in (0, 1, -1):
         for step in range(1, NEAR):
             window_copies[way, step].start()
@@ -215,7 +217,14 @@
             rows = jnp.where(sub < 3, -2.0 * base, jnp.where(sub == 3, 1.0, jnp.where(sub == 4, norm, 0.0)))
             high, middle, low = pieces(rows)
             stacked = jnp.concatenate(
-                [high, high, middle, middle, high, low, jnp.zeros((128 - SPLIT_ROWS, 128), F32)], axis=0
+                [
+                    jnp.where(sub < 5, high, pltpu.roll(low, 5, 0)),
+                    jnp.where(sub < 4, high, jnp.where(sub == 4, low, pltpu.roll(high, 5, 0))),
+                    jnp.where(sub == 3, 1.0, jnp.where(sub < 5, middle, 0.0)),
+                    jnp.where(sub < 3, middle, 0.0),
+                    jnp.zeros((128 - SPLIT_ROWS, 128), F32),
+                ],
+                axis=0,
             )
             tsplit[2 * pair + half] = stacked.T[:, 0:SPLIT_ROWS].astype(BF16)
         return carry
@@ -233,7 +242,15 @@
                 norm = extended(base)
                 rows = jnp.where(sub < 3, base, jnp.where(sub == 3, norm, jnp.where(sub == 4, 1.0, 0.0)))
                 high, middle, low = pieces(rows)
-                stacked = jnp.concatenate([high, middle, high, middle, low, high], axis=0)
+                stacked = jnp.concatenate(
+                    [
+                        jnp.where(sub < 5, high, pltpu.roll(high, 5, 0)),
+                        jnp.where(sub < 4, middle, jnp.where(sub == 4, 1.0, pltpu.roll(low, 5, 0))),
+                        jnp.where(sub < 3, high, jnp.where(sub == 3, low, jnp.where(sub == 4, 1.0, 0.0))),
+                        jnp.where(sub < 3, middle, 0.0),
+                    ],
+                    axis=0,
+                )
                 split[2 * pair + half, :, lanes] = stacked.astype(BF16)
                 weights[2 * pair + half, at] = jnp.broadcast_to(base[3:4], (8, 128))
             return carry
@@ -361,7 +378,35 @@
             window_copies[way, step].wait_recv()
     for j in range(3):
         prepare_sources(wins[j + 1], split3, wb3, j, slice(128 * j, 128 * j + 128))
-    near_slots(0, 10, split3, wb3, 3, False, 2)
+    near_slots(0, 6, split3, wb3, 3, False, 2)
+
+    for copy in l_copies:
+        copy.wait_recv()
+
+    def one_far(slot, carry):
+        target = [ftarget[c * CAP + slot] for c in range(3)]
+        running = jnp.zeros((64, 64), F32)
+        for k in range(2):
+            index = far_ref[k, slot]
+            index = jnp.where(index < 0, 3 * CAP, index)
+            squared = jnp.zeros((64, 64), F32)
+            for c in range(3):
+                spacing = target[c] - farwin[c, pl.ds(index, 1), :]
+                squared = squared + spacing * spacing
+            running = running + decay(squared) * farwin[3, pl.ds(index, 1), :]
+        return jnp.where(lanes64 == slot, jnp.sum(running, axis=1, keepdims=True), carry)
+
+    near_slots(6, 10, split3, wb3, 3, False, 4, inline=True)
+    far_columns = jnp.zeros((64, 128), F32)
+    for slot in range(CAP):
+        far_columns = one_far(slot, far_columns)
+    fbuf[near] = padded_square(far_columns).T[0:CAP, 0:64] * AMPLITUDE
+    f_copies = []
+    for step in range(1, NEAR):
+        copy = send_to(fbuf.at[near], fbuf.at[near], f_s.at[step - 1], f_r.at[step - 1], leaf, near_at(step))
+        copy.start()
+        f_copies.append(copy)
+
 
     @pl.loop(1, PLANE)
     def _(step):
@@ -401,34 +446,7 @@
         copy.start()
         g_copies.append(copy)
 
-    near_slots(10, 14, split3, wb3, 3, False, 2)
-
-    for copy in l_copies:
-        copy.wait_recv()
-
-    def one_far(slot, carry):
-        target = [ftarget[c * CAP + slot] for c in range(3)]
-        running = jnp.zeros((64, 64), F32)
-        for k in range(2):
-            index = far_ref[k, slot]
-            index = jnp.where(index < 0, 3 * CAP, index)
-            squared = jnp.zeros((64, 64), F32)
-            for c in range(3):
-                spacing = target[c] - farwin[c, pl.ds(index, 1), :]
-                squared = squared + spacing * spacing
-            running = running + decay(squared) * farwin[3, pl.ds(index, 1), :]
-        return jnp.where(lanes64 == slot, jnp.sum(running, axis=1, keepdims=True), carry)
-
-    near_slots(14, 18, split3, wb3, 3, False, 4, inline=True)
-    far_columns = jnp.zeros((64, 128), F32)
-    for slot in range(CAP):
-        far_columns = one_far(slot, far_columns)
-    fbuf[near] = padded_square(far_columns).T[0:CAP, 0:64] * AMPLITUDE
-    f_copies = []
-    for step in range(1, NEAR):
-        copy = send_to(fbuf.at[near], fbuf.at[near], f_s.at[step - 1], f_r.at[step - 1], leaf, near_at(step))
-        copy.start()
-        f_copies.append(copy)
+    near_slots(10, 20, split3, wb3, 3, False, 2)
 
     @pl.loop(1, PLANES)
     def _(step):
@@ -436,7 +454,7 @@
 
     for copy in g_copies:
         copy.wait_recv()
-    near_slots(18, 22, split3, wb3, 3, False, 4, inline=True)
+    near_slots(20, 22, split3, wb3, 3, False, 2, inline=True)
     targets[...] = jnp.zeros((128, 128), F32)
     for level in range(LEVELS):
         first = place // 2 ** level * 2 ** level
@@ -505,8 +523,6 @@
     image = jnp.where(
         occupied, noise_ref[...] * direction + AMPLITUDE * near_rows[...] + far_vals[...], 0.0
     )
-    kept_sol_ref[...] = jnp.where(occupied, sol_ref[...], 0.0)
-    kept_res_ref[...] = residual
     tile = jnp.zeros((8, 128), F32)
     for number, product in enumerate(
         (residual * residual, direction * image, residual * image, image * image)
@@ -521,20 +537,42 @@
     mine = plane * NEAR + near
     hop1[mine] = row
     hop_copies = []
-    for depth in range(PLANES):
-        for step in range(NEAR):
-            if depth or step:
-                at = depth * NEAR + step
-                copy = send_to(
-                    hop1.at[mine], hop1.at[mine], h1_s.at[at], h1_r.at[at], depth_peer(depth), near_at(step)
-                )
-                copy.start()
-                hop_copies.append(copy)
+    peers = [(depth, step) for depth in range(PLANES) for step in range(NEAR) if depth or step]
+    for depth, step in sorted(peers, key=lambda p: -min(p[0], PLANES - p[0]) - min(p[1], NEAR - p[1])):
+        at = depth * NEAR + step
+        copy = send_to(
+            hop1.at[mine], hop1.at[mine], h1_s.at[at], h1_r.at[at], depth_peer(depth), near_at(step)
+        )
+        copy.start()
+        hop_copies.append(copy)
+    for copy in window_copies.values():
+        copy.wait_send()
+
+    @pl.when(core == 0)
+    def _():
+        relay.wait_send()
+        for level in (2, 3, 4):
+            @pl.when(lax.rem(across, 2 ** (level - 1)) == 0)
+            def _(level=level):
+                for span, copy in pair_copies:
+                    if span == 2 ** (level - 1):
+                        copy.wait_send()
+
+    for copy in c_copies + l_copies + g_copies + f_copies:
+        copy.wait_send()
+
+    @pl.loop(1, PLANE)
+    def _(step):
+        a_copy(step).wait_send()
+
+    @pl.loop(1, PLANES)
+    def _(step):
+        b_copy(step).wait_send()
     for copy in hop_copies:
         copy.wait_recv()
     hop2[place] = jnp.sum(hop1[...], axis=0)
     last_copies = []
-    for step in range(1, PLANE):
+    for step in sorted(range(1, PLANE), key=lambda p: -min(p, PLANE - p)):
         copy = send_to(
             hop2.at[place], hop2.at[place], h2_s.at[step], h2_r.at[step], plane_peer(step), near
         )
@@ -547,34 +585,13 @@
     norm_old, curvature, mixed, image_norm = (totals[i:i + 1] for i in range(4))
     step_length = norm_old / curvature
     norm_new = norm_old - 2.0 * step_length * mixed + step_length * step_length * image_norm
-    step_ref[...] = jnp.broadcast_to(step_length, (CAP, 128))
-    res_step_ref[...] = step_length * image
-    ratio_ref[...] = jnp.broadcast_to(norm_new / norm_old, (CAP, 128))
-    kept_dir_ref[...] = direction
-
-    for copy in window_copies.values():
+    new_residual = residual - step_length * image
+    result_ref[0] = jnp.where(occupied, sol_ref[...], 0.0) + step_length * direction
+    result_ref[1] = new_residual
+    result_ref[2] = new_residual + norm_new / norm_old * direction
+
+    for copy in hop_copies + last_copies:
         copy.wait_send()
-
-    @pl.when(core == 0)
-    def _():
-        relay.wait_send()
-        for level in (2, 3, 4):
-            @pl.when(lax.rem(across, 2 ** (level - 1)) == 0)
-            def _(level=level):
-                for span, copy in pair_copies:
-                    if span == 2 ** (level - 1):
-                        copy.wait_send()
-
-    for copy in c_copies + l_copies + g_copies + f_copies + hop_copies + last_copies:
-        copy.wait_send()
-
-    @pl.loop(1, PLANE)
-    def _(step):
-        a_copy(step).wait_send()
-
-    @pl.loop(1, PLANES)
-    def _(step):
-        b_copy(step).wait_send()
 
 
 def per_device(
@@ -590,11 +607,11 @@
         positions, noise_variance, solution, residual, direction, leaf_basis, leaf_skeleton,
         leaf_transfer, box_transfer, box_skeleton.transpose(0, 2, 1, 3),
     )
-    kept_solution, kept_residual, residual_step, kept_direction, step, ratio = pl.pallas_call(
+    result = pl.pallas_call(
         kernel,
-        out_shape=(jax.ShapeDtypeStruct((CAP, 128), F32),) * 6,
+        out_shape=jax.ShapeDtypeStruct((3, CAP, 128), F32),
         in_specs=[smem] * 3 + [hbm] * len(arrays),
-        out_specs=(vmem,) * 6,
+        out_specs=vmem,
         scratch_shapes=[
             *[pltpu.VMEM(array.shape, F32) for array in arrays],
             dma((len(arrays),)),
@@ -633,8 +650,7 @@
         ),
         name="iteration",
     )(leaf_count, near_list.T, far_list.T, *arrays)
-    new_residual = kept_residual - residual_step
-    return kept_solution + step * kept_direction, new_residual, new_residual + ratio * kept_direction
+    return result[0], result[1], result[2]
 
 
 def solution(mesh):

time: 62.3 us -> 61.4 us (0.986)
  other arithmetic: 1.41 us -> 0 us
  local copies, waits for them, and re-layouts: 0 us -> 1.35 us
  Pallas kernels: 59.4 us -> 58.5 us
    add x1 -> x0, other arithmetic: 1.41 us -> none  [per_device(): new_residual + ratio * kept_direction]
    squeeze x0 -> x1, local copies, waits for them, and re-layouts: none -> 1.35 us  [per_device(): return (result[0], result[1], result[2])]
    pallas_call x1, Pallas kernels: 59.4 us -> 58.5 us  [per_device(): pl.pallas_call(kernel, out_shape=jax.ShapeDtypeStruct((3, CAP, 128), F32)...]
where the time goes in v4:
time: 61.4 us; the launch traced here: 61.1 us
  Pallas kernels  58.5 us (95%)
  local copies, waits for them, and re-layouts  1.35 us (2%)
  between operations  1.29 us (2%)
    pallas_call x1, Pallas kernels, per_device(): pl.pallas_call(kernel, out_shape=jax.ShapeDtypeStruct((3, CAP, 128), F32)...  58.5 us
    squeeze x1, local copies, waits for them, and re-layouts, per_device(): return (result[0], result[1], result[2])  1.35 us

profile of v4, /device:TPU:1, one launch (start us, length us, event | category | flops | bytes accessed | tf_op | source)
XLA Modules:
  0.0 61.1 jit_solution(7258772609347839623)
XLA Ops:
  1.3 58.5 %iteration.1 = f32[3,24,128]{2,1,0:T(8,128)} custom-call(s32[1]{0:T(128)S(6)} %copy.16.count_ref, s32[9,24]{1,0:T(8,128)} %bitcast.10, s32[2,24]{1,0:T(2,128)} %bitcast.11, f32[3,24,128]{2,1,0:T(8,128)} %pos_in.1, f32[24,128]{1,0:T(8,128)} %noise_in.1, f32[24,128]{1,0:T(8,128)} %sol_in.1, f32[24,128]{1,0:T(8,128)} %res_in.1, f32[24,128]{1,0:T(8,128)} %dir_in.1, ...), custom_call_target="tpu_custom_call" | custom-call | tf_op jit(solution)/shard_map/iteration/pallas_call | solution.py:610
  59.8 1.4 %slice_bitcast_fusion = (f32[24,128]{1,0:T(8,128)}, f32[24,128]{1,0:T(8,128)}, f32[24,128]{1,0:T(8,128)}) fusion(f32[3,24,128]{2,1,0:T(8,128)} %iteration.1), kind=kLoop, calls=%fused_computation | loop fusion | bytes 73728 | tf_op jit(solution)/shard_map/squeeze | solution.py:653
